TPU v7x, 128 devices: a whole 4x4x4 slice. The times are simulated.
128 devices in a mesh: energy: 16 (over z, y_lo, core), momentum: 8 (over y_hi, x).
Axes of the slice: x: 4, y: 4 (y_hi: 2, y_lo: 2; y = y_hi * 2 + y_lo), z: 4, core: 2. Of those that a mesh axis runs over, the one named last changes fastest.
Arguments:
- green_ret: bfloat16 [32, 16, 2, 512, 512], P('energy', 'momentum'), may hold values from -0.1875 to 0.1875
- sigma_in: bfloat16 [32, 16, 2, 512, 512], P('energy', 'momentum'), may hold values from -6 to 6
- screened: bfloat16 [128, 32, 16, 2, 2048], P(('energy', 'momentum')), may hold values from -6 to 6
- block_of_slot: int32 [128], replicated, may hold values from 0 to 127, each once
Outputs:
- green_new: bfloat16 [32, 16, 2, 512, 512], P('energy', 'momentum')
Inputs may be any that keep to these rules, and one draw needn't show every extreme that they name: block_of_slot is a permutation of the blocks 0 to 127.
All inputs are finite; a program needn't handle non-finite values.
Results may differ from a plain program's by a relative error of at most 0.0085.
Values may be sent and summed in bfloat16 or wider, within the bound.
A program may use at most 128 MiB of HBM per device.

v0:
```python
import jax
import jax.numpy as jnp
from jax import lax
from jax.sharding import PartitionSpec as P


def plain_product(left_side, right_side):
    return jnp.einsum("abij,abjl->abil", left_side, right_side, preferred_element_type=jnp.float32)


def adjoint_product(left_side, right_side):
    return jnp.einsum("abij,ablj->abil", left_side, right_side, preferred_element_type=jnp.float32)


def sandwich(green, sigma):
    green_real = green[:, :, 0]
    green_imag = green[:, :, 1]
    sigma_real = sigma[:, :, 0]
    sigma_imag = sigma[:, :, 1]
    first_real = (
        plain_product(green_real, sigma_real) - plain_product(green_imag, sigma_imag)
    ).astype(jnp.bfloat16)
    first_imag = (
        plain_product(green_real, sigma_imag) + plain_product(green_imag, sigma_real)
    ).astype(jnp.bfloat16)
    second_real = adjoint_product(first_real, green_real) + adjoint_product(first_imag, green_imag)
    second_imag = adjoint_product(first_imag, green_real) - adjoint_product(first_real, green_imag)
    return jnp.stack([second_real, second_imag], axis=2).astype(jnp.bfloat16)


def tables(length):
    counter = jnp.arange(length, dtype=jnp.int32)
    phases = counter[:, None] * counter[None, :] % length
    angles = phases.astype(jnp.float32) * (2.0 * jnp.pi / length)
    return (jnp.cos(angles), jnp.sin(angles))


def along_energy(table, values):
    return jnp.einsum("me,ekp->mkp", table, values, precision=lax.Precision.HIGH)


def along_momentum(table, values):
    return jnp.einsum("nk,mkp->mnp", table, values, precision=lax.Precision.HIGH)


def convolve(gathered, weight):
    energies = gathered.shape[0]
    momenta = gathered.shape[1]
    cos_energy, sin_energy = tables(energies)
    cos_momentum, sin_momentum = tables(momenta)
    values = gathered.astype(jnp.float32)
    value_real = values[:, :, 0]
    value_imag = values[:, :, 1]
    half_real = along_energy(cos_energy, value_real) + along_energy(sin_energy, value_imag)
    half_imag = along_energy(cos_energy, value_imag) - along_energy(sin_energy, value_real)
    spec_real = along_momentum(cos_momentum, half_real) + along_momentum(sin_momentum, half_imag)
    spec_imag = along_momentum(cos_momentum, half_imag) - along_momentum(sin_momentum, half_real)
    weight_real = weight[:, :, 0].astype(jnp.float32)
    weight_imag = weight[:, :, 1].astype(jnp.float32)
    times_real = spec_real * weight_real - spec_imag * weight_imag
    times_imag = spec_real * weight_imag + spec_imag * weight_real
    back_real = along_momentum(cos_momentum, times_real) - along_momentum(sin_momentum, times_imag)
    back_imag = along_momentum(cos_momentum, times_imag) + along_momentum(sin_momentum, times_real)
    final_real = along_energy(cos_energy, back_real) - along_energy(sin_energy, back_imag)
    final_imag = along_energy(cos_energy, back_imag) + along_energy(sin_energy, back_real)
    factor = 1.0 / (energies * momenta)
    return (jnp.stack([final_real, final_imag], axis=2) * factor).astype(jnp.bfloat16)


def local(green_ret, sigma_in, screened, block_of_slot):
    energies_here = green_ret.shape[0]
    momenta_here = green_ret.shape[1]
    orbitals = green_ret.shape[3]
    energy_count = lax.axis_size("energy")
    momentum_count = lax.axis_size("momentum")
    block_count = energy_count * momentum_count
    block_pairs = orbitals * orbitals // block_count
    all_energies = energies_here * energy_count
    all_momenta = momenta_here * momentum_count
    green = sandwich(green_ret, sigma_in)
    blocks = green.reshape(energies_here, momenta_here, 2, block_count, block_pairs)
    slotted = jnp.take(blocks, block_of_slot, axis=3)
    sectioned = slotted.reshape(
        energies_here, momenta_here, 2, energy_count, momentum_count, block_pairs
    )
    arrived = lax.all_to_all(
        lax.all_to_all(sectioned, "energy", split_axis=3, concat_axis=0, tiled=True),
        "momentum",
        split_axis=4,
        concat_axis=1,
        tiled=True,
    )
    gathered = arrived.reshape(all_energies, all_momenta, 2, block_pairs)
    sigma_slot = convolve(gathered, screened[0])
    outgoing = sigma_slot.reshape(all_energies, all_momenta, 2, 1, 1, block_pairs)
    received = lax.all_to_all(
        lax.all_to_all(outgoing, "energy", split_axis=0, concat_axis=3, tiled=True),
        "momentum",
        split_axis=1,
        concat_axis=4,
        tiled=True,
    )
    received = received.reshape(energies_here, momenta_here, 2, block_count, block_pairs)
    inverse = (
        jnp.zeros((block_count,), jnp.int32)
        .at[block_of_slot]
        .set(jnp.arange(block_count, dtype=jnp.int32))
    )
    restored = jnp.take(received, inverse, axis=3)
    sigma_new = restored.reshape(energies_here, momenta_here, 2, orbitals, orbitals)
    return sandwich(green_ret, sigma_new)


def solution(mesh):
    in_specs = (
        P("energy", "momentum", None, None, None),
        P("energy", "momentum", None, None, None),
        P(("energy", "momentum"), None, None, None, None),
        P(),
    )
    out_specs = P("energy", "momentum", None, None, None)
    return jax.shard_map(local, mesh=mesh, in_specs=in_specs, out_specs=out_specs, check_vma=False)
```

profile of v0, /device:TPU:30, one launch (start us, length us, event | category | flops | bytes accessed | tf_op | source)
XLA Modules:
  0.0 469.2 jit_solution(4596085599155014785)
XLA Ops:
  0.0 3.6 fusion.42
  9.8 3.3 fusion.52
  13.1 2.6 add_convert_fusion.2
  15.8 13.2 %stack.39 = bf16[2,2,1,128,2048]{4,2,3,1,0:T(2,128)(2,1)} reshape(bf16[2,2,512,512]{3,2,1,0:T(8,128)(2,1)} %add_convert_fusion.2) | data formatting | bytes 4194304 | tf_op jit(solution)/shard_map/stack | solution.py:28
  28.9 5.4 %subtract_convert_fusion.2 = bf16[2,2,512,512]{3,2,1,0:T(8,128)(2,1)} fusion(f32[2,2,512,512]{3,2,1,0:T(8,128)} %fusion.52, bf16[2,2,512,512]{3,2,1,0:T(8,128)(2,1)S(1)} %subtract_convert_fusion.3, bf16[2,2,2,512,512]{4,3,2,1,0:T(8,128)(2,1)} %param.6), kind=kOutput, calls=%fused_computation.26 | convolution fusion | flops 1075838976 | bytes 10485760 | tf_op jit(solution)/shard_map/abij,ablj->abil/dot_general | solution.py:12
  34.3 12.7 %stack.40 = bf16[2,2,1,128,2048]{4,2,3,1,0:T(2,128)(2,1)} reshape(bf16[2,2,512,512]{3,2,1,0:T(8,128)(2,1)} %subtract_convert_fusion.2) | data formatting | bytes 4194304 | tf_op jit(solution)/shard_map/stack | solution.py:28
  47.0 11.0 %pad_maximum_fusion = bf16[2,2,2,128,2048]{4,2,3,1,0:T(2,128)(2,1)} fusion(bf16[2,2,1,128,2048]{4,2,3,1,0:T(2,128)(2,1)} %stack.40, bf16[2,2,1,128,2048]{4,2,3,1,0:T(2,128)(2,1)} %stack.39), kind=kLoop, calls=%fused_computation.13 | loop fusion | flops 8388608 | bytes 8388608 | tf_op jit(solution)/shard_map/stack | solution.py:28
  58.0 14.0 %gather_fusion = bf16[128,2,2,2,2048]{4,3,2,1,0:T(2,128)(2,1)} fusion(bf16[2,2,2,128,2048]{4,2,3,1,0:T(2,128)(2,1)} %pad_maximum_fusion, s32[1024]{0:T(1024)S(1)} %pad_clamp_fusion.1), kind=kCustom, calls=%fused_computation.clone | custom fusion | bytes 8389120 | tf_op jit(solution)/shard_map/jit(_take)/gather | solution.py:82
  72.0 6.0 %broadcast_select_fusion.1 = bf16[128,2,2,2,2048]{4,3,2,1,0:T(2,128)(2,1)S(1)} fusion(bf16[128,2,2,2,2048]{4,3,2,1,0:T(2,128)(2,1)} %gather_fusion, pred[128]{0:T(512)(128)(4,1)S(1)} %compare_and_fusion.1), kind=kLoop, calls=%fused_computation.6 | loop fusion | flops 2097152 | bytes 8388736 | tf_op jit(solution)/shard_map/jit(_take)/select_n | solution.py:82
  78.0 55.8 %all_to_all.66 = bf16[2,2,2,16,8,2048]{5,2,1,0,4,3:T(2,128)(2,1)} all-to-all(bf16[2,2,2,16,8,2048]{5,2,1,0,4,3:T(2,128)(2,1)S(1)} %bitcast.212), channel_id=1, replica_groups=mesh['energy'=16,'momentum'=8] {'energy'}, dimensions={3} | all-to-all | bytes 8388608 | tf_op jit(solution)/shard_map/all_to_all | solution.py:87
  133.9 8.9 %copy.82 = bf16[16,2,2,2,1,8,2048]{6,1,0,2,3,5,4:T(2,128)(2,1)} copy(bf16[16,2,2,2,1,8,2048]{6,3,2,1,5,0,4:T(2,128)(2,1)} %bitcast.213) | data formatting | bytes 8388608 | tf_op jit(solution)/shard_map/all_to_all | solution.py:87
  142.8 7.3 %all_to_all.51 = bf16[32,2,2,1,8,2048]{5,0,1,2,3,4:T(8,128)(2,1)} reshape(bf16[16,2,2,2,1,8,2048]{6,1,0,2,3,5,4:T(2,128)(2,1)} %copy.82) | data formatting | bytes 8388608 | tf_op jit(solution)/shard_map/all_to_all | solution.py:87
  150.0 7.2 %all-to-all-start.1 = ((bf16[32,2,2,1,8,2048]{5,0,1,2,3,4:T(8,128)(2,1)}), bf16[32,2,2,1,8,2048]{5,0,1,2,3,4:T(8,128)(2,1)}, u32[]{:S(2)}, u32[]{:S(2)}) async-start(bf16[32,2,2,1,8,2048]{5,0,1,2,3,4:T(8,128)(2,1)} %all_to_all.51), calls=%async_computation.1 | async-start | bytes 8388608 | tf_op jit(solution)/shard_map/all_to_all | solution.py:86
  157.2 6.1 %copy.145 = bf16[1,32,16,2,2048]{4,2,1,3,0:T(8,128)(2,1)} copy(bf16[1,32,16,2,2048]{4,3,2,1,0:T(2,128)(2,1)} %param.8) | data formatting | bytes 8388608 | tf_op args[2]
  163.3 55.7 %all-to-all-done.1 = bf16[32,2,2,1,8,2048]{5,0,1,2,3,4:T(8,128)(2,1)} async-done(((bf16[32,2,2,1,8,2048]{5,0,1,2,3,4:T(8,128)(2,1)}), bf16[32,2,2,1,8,2048]{5,0,1,2,3,4:T(8,128)(2,1)}, u32[]{:S(2)}, u32[]{:S(2)}) %all-to-all-start.1) | async-done | bytes 4194336 | tf_op jit(solution)/shard_map/all_to_all | solution.py:86
  219.0 2.5 copy.83
  225.6 4.4 fusion.14
  229.9 4.8 %fusion.12 = f32[32,2048,16]{1,2,0:T(8,128)S(1)} fusion(f32[32,16,2048]{2,0,1:T(8,128)S(1)} %convolution_subtract_fusion), kind=kOutput, calls=%fused_computation.39 | convolution fusion | flops 100666880 | bytes 8388608 | tf_op jit(solution)/shard_map/nk,mkp->mnp/dot_general | solution.py:43
  236.1 4.8 %fusion.20 = f32[32,2048,16]{1,2,0:T(8,128)S(1)} fusion(f32[32,2048,16]{1,2,0:T(8,128)S(1)} %fusion.14, f32[32,16,2048]{2,0,1:T(8,128)S(1)} %convolution_add_fusion), kind=kOutput, calls=%fused_computation.47 | convolution fusion | flops 101715456 | bytes 12582912 | tf_op jit(solution)/shard_map/nk,mkp->mnp/dot_general | solution.py:43
  241.0 4.6 fusion.23
  245.6 3.3 fusion.109
  248.9 3.3 fusion.107
  252.2 3.8 add_bitcast_fusion.1
  256.0 4.6 fusion.6
  260.5 4.4 fusion.4
  265.0 3.8 subtract_bitcast_fusion.1
  268.7 4.7 subtract_bitcast_fusion
  273.4 4.2 add_bitcast_fusion
  278.7 2.3 copy.93
  281.0 52.9 %all_to_all.67 = bf16[32,16,2,1,1,2048]{5,1,4,3,2,0:T(8,128)(2,1)S(1)} all-to-all(bf16[32,16,2,1,1,2048]{5,1,4,3,2,0:T(8,128)(2,1)S(1)} %copy.93), channel_id=1, replica_groups=mesh['energy'=16,'momentum'=8] {'energy'}, dimensions={0} | all-to-all | bytes 8388608 | tf_op jit(solution)/shard_map/all_to_all | solution.py:97
  333.9 4.3 copy.144
  338.2 6.9 %all-to-all-start.3 = ((bf16[2,16,2,16,1,2048]{5,3,2,0,4,1:T(8,128)(2,1)}), bf16[2,16,2,16,1,2048]{5,3,2,0,4,1:T(8,128)(2,1)}, u32[]{:S(2)}, u32[]{:S(2)}) async-start(bf16[2,16,2,16,1,2048]{5,3,2,0,4,1:T(8,128)(2,1)} %bitcast.211), calls=%async_computation.3 | async-start | bytes 8388608 | tf_op jit(solution)/shard_map/all_to_all | solution.py:96
  346.3 60.6 %all-to-all-done.3 = bf16[2,16,2,16,1,2048]{5,3,2,0,4,1:T(8,128)(2,1)} async-done(((bf16[2,16,2,16,1,2048]{5,3,2,0,4,1:T(8,128)(2,1)}), bf16[2,16,2,16,1,2048]{5,3,2,0,4,1:T(8,128)(2,1)}, u32[]{:S(2)}, u32[]{:S(2)}) %all-to-all-start.3) | async-done | bytes 4194336 | tf_op jit(solution)/shard_map/all_to_all | solution.py:96
  406.9 2.5 copy.95
  409.4 2.7 copy.143
  412.1 6.3 %copy.97 = bf16[2,2,2,128,2048]{4,2,3,1,0:T(2,128)(2,1)} copy(bf16[2,2,2,128,2048]{4,3,2,1,0:T(8,128)(2,1)S(1)} %bitcast.216) | data formatting | bytes 8388608 | tf_op jit(solution)/shard_map/reshape | solution.py:103
  418.5 14.2 %gather_fusion.1 = bf16[128,2,2,2,2048]{4,3,2,1,0:T(2,128)(2,1)} fusion(bf16[2,2,2,128,2048]{4,2,3,1,0:T(2,128)(2,1)} %copy.97, s32[1024]{0:T(1024)S(1)} %pad_clamp_fusion), kind=kCustom, calls=%fused_computation.1.clone | custom fusion | bytes 8389120 | tf_op jit(solution)/shard_map/jit(_take)/gather | solution.py:109
  432.7 6.0 %fusion.3 = bf16[2,2,2,128,2048]{4,2,1,0,3:T(2,128)(2,1)S(1)} fusion(bf16[128,2,2,2,2048]{4,3,2,1,0:T(2,128)(2,1)} %gather_fusion.1, pred[128]{0:T(512)(128)(4,1)S(1)} %compare_and_fusion), kind=kLoop, calls=%fused_computation.30 | loop fusion | flops 2097152 | bytes 8388736 | tf_op jit(solution)/shard_map/jit(_take)/select_n | solution.py:109
  438.7 4.3 copy.98
  443.0 7.7 %reshape.68 = bf16[2,2,2,512,512]{4,3,2,1,0:T(8,128)(2,1)} reshape(bf16[2,2,2,128,2048]{4,3,2,1,0:T(8,128)(2,1)} %copy.98) | data formatting | bytes 8388608 | tf_op jit(solution)/shard_map/reshape | solution.py:110
  450.8 3.8 fusion.50
  456.9 1.5 subtract_convert_fusion.1
  458.5 1.5 fusion.48
  459.9 1.5 add_convert_fusion.1
  461.5 1.5 fusion.44
  463.0 1.5 fusion.64
  464.5 1.5 fusion.67
  466.4 2.5 copy.105
  (31 shorter events, 16.5 us)
Async XLA Ops:
  0.0 3.6 copy-start
  0.0 4.7 %copy-start.4 = (bf16[2,2,2,512,512]{4,3,2,1,0:T(8,128)(2,1)S(1)}, bf16[2,2,2,512,512]{4,3,2,1,0:T(8,128)(2,1)}, u32[]{:S(2)}) copy-start(bf16[2,2,2,512,512]{4,3,2,1,0:T(8,128)(2,1)} %param.7) | copy-start | bytes 12582916
  4.7 1.3 copy-start.5
  150.0 69.0 %all-to-all-start.1 = ((bf16[32,2,2,1,8,2048]{5,0,1,2,3,4:T(8,128)(2,1)}), bf16[32,2,2,1,8,2048]{5,0,1,2,3,4:T(8,128)(2,1)}, u32[]{:S(2)}, u32[]{:S(2)}) async-start(bf16[32,2,2,1,8,2048]{5,0,1,2,3,4:T(8,128)(2,1)} %all_to_all.51), calls=%async_computation.1 | async-start | bytes 8388608 | tf_op jit(solution)/shard_map/all_to_all | solution.py:86
  240.9 4.7 copy-start.2
  338.2 68.7 %all-to-all-start.3 = ((bf16[2,16,2,16,1,2048]{5,3,2,0,4,1:T(8,128)(2,1)}), bf16[2,16,2,16,1,2048]{5,3,2,0,4,1:T(8,128)(2,1)}, u32[]{:S(2)}, u32[]{:S(2)}) async-start(bf16[2,16,2,16,1,2048]{5,3,2,0,4,1:T(8,128)(2,1)} %bitcast.211), calls=%async_computation.3 | async-start | bytes 8388608 | tf_op jit(solution)/shard_map/all_to_all | solution.py:96
  450.8 3.8 copy-start.1
  450.8 4.7 %copy-start.3 = (bf16[2,2,2,512,512]{4,3,2,1,0:T(8,128)(2,1)S(1)}, bf16[2,2,2,512,512]{4,3,2,1,0:T(8,128)(2,1)}, u32[]{:S(2)}) copy-start(bf16[2,2,2,512,512]{4,3,2,1,0:T(8,128)(2,1)} %reshape.68) | copy-start | bytes 12582916
where the time goes:
time: 476 us; the launch traced here: 469 us
  waiting for transfers between devices  116 us (24%)
  local copies, waits for them, and re-layouts  115 us (24%)
  blocking collectives  109 us (23%)
  matrix products  90.4 us (19%)
  other arithmetic  24.4 us (5%)
  starting transfers between devices  14.1 us (3%)
    all_to_all x1, waiting for transfers between devices, local(): lax.all_to_all(lax.all_to_all(outgoing, 'energy', split_axis=0, concat_ax...  60.6 us
    all_to_all x1, blocking collectives, local(): lax.all_to_all(sectioned, 'energy', split_axis=3, concat_axis=0, tiled=True)  55.8 us
    all_to_all x1, waiting for transfers between devices, local(): lax.all_to_all(lax.all_to_all(sectioned, 'energy', split_axis=3, concat_a...  55.7 us
    all_to_all x1, blocking collectives, local(): lax.all_to_all(outgoing, 'energy', split_axis=0, concat_axis=3, tiled=True)  52.9 us
    dot_general x8, matrix products, along_momentum(): jnp.einsum('nk,mkp->mnp', table, values, precision=lax.Precision.HIGH)  32.7 us
    another operation x3, local copies, waits for them, and re-layouts, sandwich(): return jnp.stack([second_real, second_imag], axis=2).astype(jnp.bfloat16)  28.3 us
    dot_general x8, matrix products, along_energy(): jnp.einsum('me,ekp->mkp', table, values, precision=lax.Precision.HIGH)  23.3 us
    dot_general x8, matrix products, adjoint_product(): jnp.einsum('abij,ablj->abil', left_side, right_side, preferred_element_ty...  18.6 us
  transfers between devices with their start and end apart: 2, of which 2 were waited for; matrix products, arithmetic and copies ran while one was open for 2% of the time, Pallas kernels for 0%

commit v1 on v0

--- a/solution.py
+++ b/solution.py
@@ -1,6 +1,10 @@
+import functools
+
 import jax
 import jax.numpy as jnp
 from jax import lax
+from jax.experimental import pallas as pl
+from jax.experimental.pallas import tpu as pltpu
 from jax.sharding import PartitionSpec as P
 
 
@@ -67,47 +71,98 @@
     return (jnp.stack([final_real, final_imag], axis=2) * factor).astype(jnp.bfloat16)
 
 
+def exchange_kernel(src, dst, send_sem, recv_sem, own_sem):
+    e = lax.axis_index("energy")
+    m = lax.axis_index("momentum")
+    me = e * 8 + m
+
+    def partner(i):
+        core, z, y, x = i % 2, (i // 2) % 4, (i // 8) % 4, i // 32
+        my_y = (m // 4) * 2 + (e // 2) % 2
+        to_x = (m % 4 + x) % 4
+        to_y = (my_y + y) % 4
+        to_z = (e // 4 + z) % 4
+        to_core = (e % 2 + core) % 2
+        return to_z * 4 + (to_y % 2) * 2 + to_core, (to_y // 2) * 4 + to_x
+
+    barrier = pltpu.get_barrier_semaphore()
+
+    def greet(i, _):
+        pl.semaphore_signal(barrier, inc=1, device_id=partner(i), device_id_type=pl.DeviceIdType.MESH)
+        return 0
+
+    lax.fori_loop(1, 128, greet, 0)
+    pl.semaphore_wait(barrier, 127)
+    for chunk in range(4):
+        def send(i, _):
+            to = partner(i)
+            pltpu.make_async_remote_copy(
+                src.at[chunk, to[0] * 8 + to[1]],
+                dst.at[chunk, me],
+                send_sem.at[chunk],
+                recv_sem.at[chunk],
+                device_id=to,
+                device_id_type=pl.DeviceIdType.MESH,
+            ).start()
+            return 0
+
+        lax.fori_loop(1, 128, send, 0)
+        pltpu.make_async_copy(src.at[chunk, me], dst.at[chunk, me], own_sem.at[chunk]).start()
+    for chunk in range(4):
+        pltpu.make_async_copy(src.at[chunk, me], dst.at[chunk, me], own_sem.at[chunk]).wait()
+        some = pl.ds(0, 127)
+        pltpu.make_async_copy(src.at[chunk, some], dst.at[chunk, some], recv_sem.at[chunk]).wait()
+        pltpu.make_async_copy(src.at[chunk, some], dst.at[chunk, some], send_sem.at[chunk]).wait()
+
+
+def exchange(values):
+    return pl.pallas_call(
+        exchange_kernel,
+        out_shape=jax.ShapeDtypeStruct(values.shape, values.dtype),
+        in_specs=[pl.BlockSpec(memory_space=pltpu.VMEM)],
+        out_specs=pl.BlockSpec(memory_space=pltpu.VMEM),
+        scratch_shapes=[pltpu.SemaphoreType.DMA((4,))] * 3,
+        compiler_params=pltpu.CompilerParams(
+            collective_id=0, has_side_effects=True, vmem_limit_bytes=20 << 20
+        ),
+    )(values)
+
+
+def reorder_kernel(inverse, order, src, dst):
+    def move(slot, _):
+        block = order[slot]
+        if inverse:
+            dst[:, block] = src[:, slot]
+        else:
+            dst[:, slot] = src[:, block]
+        return 0
+
+    lax.fori_loop(0, 128, move, 0)
+
+
+def reorder(values, order, inverse):
+    return pl.pallas_call(
+        functools.partial(reorder_kernel, inverse),
+        out_shape=jax.ShapeDtypeStruct(values.shape, values.dtype),
+        in_specs=[
+            pl.BlockSpec(memory_space=pltpu.SMEM),
+            pl.BlockSpec(memory_space=pltpu.VMEM),
+        ],
+        out_specs=pl.BlockSpec(memory_space=pltpu.VMEM),
+        compiler_params=pltpu.CompilerParams(vmem_limit_bytes=20 << 20),
+    )(order, values)
+
+
 def local(green_ret, sigma_in, screened, block_of_slot):
-    energies_here = green_ret.shape[0]
-    momenta_here = green_ret.shape[1]
-    orbitals = green_ret.shape[3]
-    energy_count = lax.axis_size("energy")
-    momentum_count = lax.axis_size("momentum")
-    block_count = energy_count * momentum_count
-    block_pairs = orbitals * orbitals // block_count
-    all_energies = energies_here * energy_count
-    all_momenta = momenta_here * momentum_count
     green = sandwich(green_ret, sigma_in)
-    blocks = green.reshape(energies_here, momenta_here, 2, block_count, block_pairs)
-    slotted = jnp.take(blocks, block_of_slot, axis=3)
-    sectioned = slotted.reshape(
-        energies_here, momenta_here, 2, energy_count, momentum_count, block_pairs
-    )
-    arrived = lax.all_to_all(
-        lax.all_to_all(sectioned, "energy", split_axis=3, concat_axis=0, tiled=True),
-        "momentum",
-        split_axis=4,
-        concat_axis=1,
-        tiled=True,
-    )
-    gathered = arrived.reshape(all_energies, all_momenta, 2, block_pairs)
+    blocks = green.reshape(2, 2, 2, 128, 2048).transpose(0, 1, 3, 2, 4).reshape(4, 128, 32, 128)
+    outgoing = reorder(blocks, block_of_slot, False)
+    arrived = exchange(outgoing).reshape(2, 2, 16, 8, 2, 2048)
+    gathered = arrived.transpose(2, 0, 3, 1, 4, 5).reshape(32, 16, 2, 2048)
     sigma_slot = convolve(gathered, screened[0])
-    outgoing = sigma_slot.reshape(all_energies, all_momenta, 2, 1, 1, block_pairs)
-    received = lax.all_to_all(
-        lax.all_to_all(outgoing, "energy", split_axis=0, concat_axis=3, tiled=True),
-        "momentum",
-        split_axis=1,
-        concat_axis=4,
-        tiled=True,
-    )
-    received = received.reshape(energies_here, momenta_here, 2, block_count, block_pairs)
-    inverse = (
-        jnp.zeros((block_count,), jnp.int32)
-        .at[block_of_slot]
-        .set(jnp.arange(block_count, dtype=jnp.int32))
-    )
-    restored = jnp.take(received, inverse, axis=3)
-    sigma_new = restored.reshape(energies_here, momenta_here, 2, orbitals, orbitals)
+    back = sigma_slot.reshape(16, 2, 8, 2, 2, 2048).transpose(1, 3, 0, 2, 4, 5).reshape(4, 128, 32, 128)
+    restored = reorder(exchange(back), block_of_slot, True).reshape(2, 2, 128, 2, 2048)
+    sigma_new = restored.transpose(0, 1, 3, 2, 4).reshape(2, 2, 2, 512, 512)
     return sandwich(green_ret, sigma_new)
 
 

time: 476 us -> 392 us (0.82)
  the two profiles are of different devices: /device:TPU:30 before, /device:TPU:1 now
where the time goes in v1:
time: 392 us; the launch traced here: 385 us
  Pallas kernels  137 us (35%)
  local copies, waits for them, and re-layouts  130 us (33%)
  matrix products  96 us (24%)
  other arithmetic  21.7 us (6%)
    pallas_call x2, Pallas kernels, exchange(): pl.pallas_call(exchange_kernel, out_shape=jax.ShapeDtypeStruct(values.sha...  134 us
    dot_general x8, matrix products, along_momentum(): jnp.einsum('nk,mkp->mnp', table, values, precision=lax.Precision.HIGH)  32.9 us
    dot_general x8, matrix products, along_energy(): jnp.einsum('me,ekp->mkp', table, values, precision=lax.Precision.HIGH)  31.1 us
    another operation x4, local copies, waits for them, and re-layouts, convolve(): jnp.stack([final_real, final_imag], axis=2) * factor  28.9 us
    another operation x3, local copies, waits for them, and re-layouts, sandwich(): return jnp.stack([second_real, second_imag], axis=2).astype(jnp.bfloat16)  28.1 us
    dot_general x8, matrix products, adjoint_product(): jnp.einsum('abij,ablj->abil', left_side, right_side, preferred_element_ty...  16.3 us
    dot_general x8, matrix products, plain_product(): jnp.einsum('abij,abjl->abil', left_side, right_side, preferred_element_ty...  15.7 us
    unnamed x33, local copies, waits for them, and re-layouts  13.6 us

profile of v1, /device:TPU:1, one launch (start us, length us, event | category | flops | bytes accessed | tf_op | source)
XLA Modules:
  0.0 385.3 jit_solution(8345391196919770522)
XLA Ops:
  0.0 3.6 fusion.44
  11.1 2.6 add_convert_fusion.2
  13.8 12.9 %stack.39 = bf16[2,2,1,128,2048]{4,2,3,1,0:T(2,128)(2,1)} reshape(bf16[2,2,512,512]{3,2,1,0:T(8,128)(2,1)} %add_convert_fusion.2) | data formatting | bytes 4194304 | tf_op jit(solution)/shard_map/stack | solution.py:32
  26.7 3.7 fusion.54
  30.3 2.7 subtract_convert_fusion.2
  33.0 12.7 %stack.40 = bf16[2,2,1,128,2048]{4,2,3,1,0:T(2,128)(2,1)} reshape(bf16[2,2,512,512]{3,2,1,0:T(8,128)(2,1)} %subtract_convert_fusion.2) | data formatting | bytes 4194304 | tf_op jit(solution)/shard_map/stack | solution.py:32
  45.7 10.9 %maximum_bitcast_fusion = bf16[2,2,128,2,2048]{4,3,2,1,0:T(2,128)(2,1)} fusion(bf16[2,2,1,128,2048]{4,2,3,1,0:T(2,128)(2,1)} %stack.40, bf16[2,2,1,128,2048]{4,2,3,1,0:T(2,128)(2,1)} %stack.39), kind=kLoop, calls=%fused_computation.8 | loop fusion | flops 8388608 | bytes 8388608 | tf_op jit(solution)/shard_map/transpose | solution.py:158
  56.7 7.6 %reshape.34.src = bf16[4,128,32,128]{3,2,1,0:T(8,128)(2,1)} reshape(bf16[2,2,128,2,2048]{4,3,2,1,0:T(2,128)(2,1)} %maximum_bitcast_fusion) | data formatting | bytes 8388608 | tf_op jit(solution)/shard_map/reshape | solution.py:158
  64.3 2.2 copy-done
  67.9 69.2 %shard_map.47 = bf16[4,128,32,128]{3,2,1,0:T(8,128)(2,1)S(1)} custom-call(bf16[4,128,32,128]{3,2,1,0:T(8,128)(2,1)S(1)} %shard_map.46.src), custom_call_target="tpu_custom_call" | custom-call | tf_op jit(solution)/shard_map/pallas_call | solution.py:119
  137.1 2.0 copy-done.1
  139.1 6.9 %reshape.35 = bf16[2,2,16,8,2,2048]{5,4,3,2,1,0:T(2,128)(2,1)} reshape(bf16[4,128,32,128]{3,2,1,0:T(8,128)(2,1)} %copy-done.1) | data formatting | bytes 8388608 | tf_op jit(solution)/shard_map/reshape | solution.py:160
  146.0 8.7 %copy.34 = bf16[16,2,8,2,2,2048]{5,1,0,3,2,4:T(2,128)(2,1)} copy(bf16[16,2,8,2,2,2048]{5,4,2,0,3,1:T(2,128)(2,1)} %bitcast.195) | data formatting | bytes 8388608 | tf_op jit(solution)/shard_map/transpose | solution.py:161
  154.7 7.6 %reshape.36 = bf16[32,16,2,2048]{3,0,1,2:T(8,128)(2,1)} reshape(bf16[16,2,8,2,2,2048]{5,1,0,3,2,4:T(2,128)(2,1)} %copy.34) | data formatting | bytes 8388608 | tf_op jit(solution)/shard_map/reshape | solution.py:161
  162.3 3.0 fusion.60
  168.0 1.5 convolution_subtract_fusion
  169.5 4.4 %fusion.14 = f32[32,2048,16]{1,2,0:T(8,128)S(1)} fusion(f32[32,16,2048]{2,0,1:T(8,128)S(1)} %convolution_subtract_fusion), kind=kOutput, calls=%fused_computation.33 | convolution fusion | flops 100666880 | bytes 8388608 | tf_op jit(solution)/shard_map/nk,mkp->mnp/dot_general | solution.py:47
  173.9 5.0 %fusion.20 = f32[32,2048,16]{1,2,0:T(8,128)S(1)} fusion(f32[32,2048,16]{1,2,0:T(8,128)S(1)} %fusion.14, f32[32,16,2048]{2,0,1:T(8,128)S(1)} %convolution_add_fusion), kind=kOutput, calls=%fused_computation.39 | convolution fusion | flops 101715456 | bytes 12582912 | tf_op jit(solution)/shard_map/nk,mkp->mnp/dot_general | solution.py:47
  178.9 4.4 %fusion.12 = f32[32,2048,16]{1,2,0:T(8,128)S(1)} fusion(f32[32,16,2048]{2,0,1:T(8,128)S(1)} %convolution_subtract_fusion), kind=kOutput, calls=%fused_computation.31 | convolution fusion | flops 100666880 | bytes 8388608 | tf_op jit(solution)/shard_map/nk,mkp->mnp/dot_general | solution.py:47
  183.3 4.8 %fusion.23 = f32[32,2048,16]{1,2,0:T(8,128)S(1)} fusion(f32[32,2048,16]{1,2,0:T(8,128)S(1)} %fusion.12, f32[32,16,2048]{2,0,1:T(8,128)S(1)} %convolution_add_fusion), kind=kOutput, calls=%fused_computation.40 | convolution fusion | flops 101715456 | bytes 12582912 | tf_op jit(solution)/shard_map/nk,mkp->mnp/dot_general | solution.py:47
  188.1 1.9 copy.91
  190.0 3.5 fusion.111
  193.5 3.8 subtract_bitcast_fusion
  197.3 3.3 fusion.109
  200.6 3.8 add_bitcast_fusion
  204.4 4.7 %fusion.6 = f32[32,16,2048]{2,0,1:T(8,128)S(1)} fusion(f32[32,16,2048]{2,1,0:T(8,128)S(1)} %add_bitcast_fusion), kind=kOutput, calls=%fused_computation.25 | convolution fusion | flops 201340928 | bytes 8388608 | tf_op jit(solution)/shard_map/me,ekp->mkp/dot_general | solution.py:43
  209.2 6.3 %fusion.26 = f32[32,16,2048]{2,0,1:T(8,128)} fusion(f32[32,16,2048]{2,0,1:T(8,128)S(1)} %fusion.6, f32[32,16,2048]{2,1,0:T(8,128)S(1)} %subtract_bitcast_fusion), kind=kOutput, calls=%fused_computation.41 | convolution fusion | flops 202389504 | bytes 12582912 | tf_op jit(solution)/shard_map/me,ekp->mkp/dot_general | solution.py:43
  215.4 6.0 %stack.33 = f32[16,2,8,2,1,2048]{5,1,0,3,2,4:T(2,128)} reshape(f32[32,16,2048]{2,0,1:T(8,128)} %fusion.26) | data formatting | bytes 8388608 | tf_op jit(solution)/shard_map/stack | solution.py:71
  221.4 8.5 %copy.44 = f32[16,2,8,2,1,2048]{5,4,2,0,3,1:T(1,128)} copy(f32[16,2,8,2,1,2048]{5,1,0,3,2,4:T(2,128)} %stack.33) | data formatting | bytes 8388608 | tf_op jit(solution)/shard_map/stack | solution.py:71
  229.9 6.5 %fusion.4 = f32[32,16,2048]{2,0,1:T(8,128)S(1)} fusion(f32[32,16,2048]{2,1,0:T(8,128)} %copy-done.12), kind=kOutput, calls=%fused_computation.23 | convolution fusion | flops 201340928 | bytes 8388608 | tf_op jit(solution)/shard_map/me,ekp->mkp/dot_general | solution.py:43
  236.5 6.4 %fusion.29 = f32[32,16,2048]{2,0,1:T(8,128)} fusion(f32[32,16,2048]{2,0,1:T(8,128)S(1)} %fusion.4, f32[32,16,2048]{2,1,0:T(8,128)S(1)} %copy-done.10), kind=kOutput, calls=%fused_computation.42 | convolution fusion | flops 202389504 | bytes 12582912 | tf_op jit(solution)/shard_map/me,ekp->mkp/dot_general | solution.py:43
  242.9 5.8 %stack.34 = f32[16,2,8,2,1,2048]{5,1,0,3,2,4:T(2,128)} reshape(f32[32,16,2048]{2,0,1:T(8,128)} %fusion.29) | data formatting | bytes 8388608 | tf_op jit(solution)/shard_map/stack | solution.py:71
  248.7 8.6 %copy.45 = f32[16,2,8,2,1,2048]{5,4,2,0,3,1:T(1,128)} copy(f32[16,2,8,2,1,2048]{5,1,0,3,2,4:T(2,128)} %stack.34) | data formatting | bytes 8388608 | tf_op jit(solution)/shard_map/stack | solution.py:71
  257.3 10.3 %fusion.3 = bf16[2,2,16,8,2,2048]{5,4,3,2,1,0:T(2,128)(2,1)} fusion(f32[16,2,8,2,1,2048]{5,4,2,0,3,1:T(1,128)} %copy.45, f32[16,2,8,2,1,2048]{5,4,2,0,3,1:T(1,128)} %copy.44), kind=kLoop, calls=%fused_computation.22 | loop fusion | flops 6291456 | bytes 12582912 | tf_op jit(solution)/shard_map/transpose | solution.py:163
  267.6 7.6 %reshape.37.src = bf16[4,128,32,128]{3,2,1,0:T(8,128)(2,1)} reshape(bf16[2,2,16,8,2,2048]{5,4,3,2,1,0:T(2,128)(2,1)} %fusion.3) | data formatting | bytes 8388608 | tf_op jit(solution)/shard_map/reshape | solution.py:163
  275.2 2.2 copy-done.2
  277.4 65.2 %shard_map.48.src = bf16[4,128,32,128]{3,2,1,0:T(8,128)(2,1)S(1)} custom-call(bf16[4,128,32,128]{3,2,1,0:T(8,128)(2,1)S(1)} %copy-done.2), custom_call_target="tpu_custom_call" | custom-call | tf_op jit(solution)/shard_map/pallas_call | solution.py:119
  343.9 2.0 copy-done.3
  345.9 6.9 %reshape.38 = bf16[2,2,128,2,2048]{4,3,2,1,0:T(2,128)(2,1)} reshape(bf16[4,128,32,128]{3,2,1,0:T(8,128)(2,1)} %copy-done.3) | data formatting | bytes 8388608 | tf_op jit(solution)/shard_map/reshape | solution.py:164
  352.9 6.1 %copy.90 = bf16[2,2,128,2,2048]{4,2,3,1,0:T(8,128)(2,1)} copy(bf16[2,2,128,2,2048]{4,3,2,1,0:T(2,128)(2,1)} %reshape.38) | data formatting | bytes 8388608 | tf_op jit(solution)/shard_map/reshape | solution.py:164
  358.9 7.8 %reshape.39 = bf16[2,2,2,512,512]{4,3,2,1,0:T(8,128)(2,1)} reshape(bf16[2,2,2,128,2048]{4,3,2,1,0:T(8,128)(2,1)} %bitcast.196) | data formatting | bytes 8388608 | tf_op jit(solution)/shard_map/reshape | solution.py:165
  366.7 3.8 fusion.52
  371.4 1.5 subtract_convert_fusion.1
  373.0 1.5 fusion.50
  375.9 1.5 add_convert_fusion.1
  377.5 1.5 fusion.66
  380.5 1.5 fusion.69
  382.4 2.5 copy.53
  (39 shorter events, 17.1 us)
Async XLA Ops:
  0.0 3.6 copy-start.5
  0.0 4.7 %copy-start.14 = (bf16[2,2,2,512,512]{4,3,2,1,0:T(8,128)(2,1)S(1)}, bf16[2,2,2,512,512]{4,3,2,1,0:T(8,128)(2,1)}, u32[]{:S(2)}) copy-start(bf16[2,2,2,512,512]{4,3,2,1,0:T(8,128)(2,1)} %param.5) | copy-start | bytes 12582916
  9.8 1.3 copy-start.13
  26.7 3.7 copy-start.6
  56.7 7.6 %copy-start.4 = (s32[128]{0:T(128)S(1)}, s32[128]{0:T(128)}, u32[]{:S(2)}) copy-start(s32[128]{0:T(128)} %order.3) | copy-start | bytes 1540
  64.3 2.2 copy-start
  137.1 2.0 copy-start.1
  162.3 3.1 copy-start.8
  183.3 4.9 %copy-start.15 = (bf16[1,32,16,2,2048]{4,3,2,1,0:T(2,128)(2,1)S(1)}, bf16[1,32,16,2,2048]{4,3,2,1,0:T(2,128)(2,1)}, u32[]{:S(2)}) copy-start(bf16[1,32,16,2,2048]{4,3,2,1,0:T(2,128)(2,1)} %param.6) | copy-start | bytes 12582916
  197.3 11.9 %copy-start.9 = (f32[32,16,2048]{2,1,0:T(8,128)}, f32[32,16,2048]{2,1,0:T(8,128)S(1)}, u32[]{:S(2)}) copy-start(f32[32,16,2048]{2,1,0:T(8,128)S(1)} %subtract_bitcast_fusion) | copy-start | bytes 12582916
  204.4 4.8 %copy-start.12 = (f32[32,16,2048]{2,1,0:T(8,128)}, f32[32,16,2048]{2,1,0:T(8,128)S(1)}, u32[]{:S(2)}) copy-start(f32[32,16,2048]{2,1,0:T(8,128)S(1)} %add_bitcast_fusion) | copy-start | bytes 12582916
  229.9 6.5 %copy-start.10 = (f32[32,16,2048]{2,1,0:T(8,128)S(1)}, f32[32,16,2048]{2,1,0:T(8,128)}, u32[]{:S(2)}) copy-start(f32[32,16,2048]{2,1,0:T(8,128)} %copy-done.9) | copy-start | bytes 12582916
  275.2 2.2 copy-start.2
  343.9 2.0 copy-start.3
  366.7 3.8 copy-start.7
  366.7 4.7 %copy-start.11 = (bf16[2,2,2,512,512]{4,3,2,1,0:T(8,128)(2,1)S(1)}, bf16[2,2,2,512,512]{4,3,2,1,0:T(8,128)(2,1)}, u32[]{:S(2)}) copy-start(bf16[2,2,2,512,512]{4,3,2,1,0:T(8,128)(2,1)} %reshape.39) | copy-start | bytes 12582916

commit v2 on v1

v2 whole, which is shorter than its diff:
```python
import jax
import jax.numpy as jnp
import numpy as np
from jax import lax
from jax.experimental import pallas as pl
from jax.experimental.pallas import tpu as pltpu
from jax.sharding import PartitionSpec as P

BF = jnp.bfloat16
F32 = jnp.float32
CHUNKS = 4
WIDE = 128


def transforms():
    m, n = np.arange(16), np.arange(8)
    e, k = np.arange(16), np.arange(8)
    out = np.zeros((4, 256, 256), np.float64)
    for a in range(2):
        for b in range(2):
            steps = ((2 * m + a)[:, None, None, None] * e[None, None, :, None]) * 1.0 / 32
            steps = steps + ((2 * n + b)[None, :, None, None] * k[None, None, None, :]) * 1.0 / 16
            cos, sin = np.cos(2 * np.pi * steps), np.sin(2 * np.pi * steps)
            cols = np.zeros((2, 16, 8, 16, 8, 2))
            cols[0, ..., 0], cols[0, ..., 1] = cos, sin
            cols[1, ..., 0], cols[1, ..., 1] = -sin, cos
            cols = cols.reshape(2, 16, 8, 8, 2, 4, 2, 2).transpose(0, 1, 2, 3, 5, 4, 6, 7)
            out[2 * a + b] = cols.reshape(256, 256)
    back = out.transpose(0, 2, 1) / 512
    return jnp.asarray(out, BF), jnp.asarray(back, BF)


def swapper():
    row = np.arange(256)
    swapped = (row % 8) * 32 + (row // 8 % 4) * 8 + row // 32
    return jnp.asarray(np.arange(256)[None, :] == swapped[:, None], BF)


def dot(a, b):
    return jnp.dot(a, b, preferred_element_type=F32)


def dot_t(a, b):
    return lax.dot_general(a, b, (((1,), (1,)), ((), ())), preferred_element_type=F32)


def kernel(
    order, green, sigma, weight, forth, back, swap, out,
    g, s, w, tf, ti, sw, rows, cols, first, gbuf, gcol, stage1, got1, stage2, got2, sig, acc,
    load_sem, send1, recv1, send2, recv2, out_sem,
):
    e = lax.axis_index("energy")
    m = lax.axis_index("momentum")
    me = e * 8 + m

    def partner(i):
        core, z, y, x = i % 2, (i // 2) % 4, (i // 8) % 4, i // 32
        my_y = (m // 4) * 2 + (e // 2) % 2
        to_x = (m % 4 + x) % 4
        to_y = (my_y + y) % 4
        to_z = (e // 4 + z) % 4
        to_core = (e % 2 + core) % 2
        return to_z * 4 + (to_y % 2) * 2 + to_core, (to_y // 2) * 4 + to_x

    def load_point(pt):
        return (
            pltpu.make_async_copy(green.at[pt], g.at[pt], load_sem.at[pt]),
            pltpu.make_async_copy(sigma.at[pt], s.at[pt], load_sem.at[4 + pt]),
        )

    late = (
        pltpu.make_async_copy(swap, sw, load_sem.at[8]),
        pltpu.make_async_copy(forth, tf, load_sem.at[9]),
        pltpu.make_async_copy(back, ti, load_sem.at[10]),
        pltpu.make_async_copy(weight, w, load_sem.at[11]),
    )
    for pt in range(4):
        for copy in load_point(pt):
            copy.start()
    for copy in late:
        copy.start()

    barrier = pltpu.get_barrier_semaphore()

    def greet(i, _):
        pl.semaphore_signal(barrier, inc=1, device_id=partner(i), device_id_type=pl.DeviceIdType.MESH)
        return 0

    lax.fori_loop(1, 128, greet, 0)

    lane = lax.broadcasted_iota(jnp.int32, (128, 512), 1)
    slot = lax.broadcasted_iota(jnp.int32, (128, 512), 0)
    spread = (slot == (lane // 32) * 8 + lane % 8).astype(F32).astype(BF)
    blocks = jnp.broadcast_to(order[...].astype(F32), (8, 128)).astype(BF)
    target = dot(blocks, spread)[0:1] * 4.0
    lane1 = lax.broadcasted_iota(jnp.int32, (1, 512), 1)
    target = target + ((lane1 // 8) % 4).astype(F32)
    index = lax.broadcasted_iota(jnp.int32, (512, 512), 0).astype(F32)
    onehot = jnp.where(index == target, 1.0, 0.0)
    cols[...] = onehot.astype(BF)
    rows[...] = onehot.T.astype(BF)

    def make_first(pt, _):
        for copy in load_point(pt):
            copy.wait()
        gr, gi = g[pt, 0], g[pt, 1]
        real = dot(gr, s[pt, 0]) - dot(gi, s[pt, 1])
        imag = dot(gr, s[pt, 1]) + dot(gi, s[pt, 0])
        both = jnp.concatenate([real.astype(BF), imag.astype(BF)], axis=1)
        placed = dot(rows[...], both)
        first[pt, 0] = placed[:, :512].astype(BF)
        first[pt, 1] = placed[:, 512:].astype(BF)
        return 0

    lax.fori_loop(0, 4, make_first, 0)
    late[0].wait()
    pl.semaphore_wait(barrier, 127)

    def outward(chunk, _):
        here = pl.ds(pl.multiple_of(chunk * WIDE, WIDE), WIDE)

        def make_green(pt, _):
            side = g[pt, :, here, :].reshape(2 * WIDE, 512)
            a = dot_t(first[pt, 0], side)
            b = dot_t(first[pt, 1], side)
            gbuf[2 * pt] = (a[:, :WIDE] + b[:, WIDE:]).astype(BF)
            gbuf[2 * pt + 1] = (b[:, :WIDE] - a[:, WIDE:]).astype(BF)
            return 0

        lax.fori_loop(0, 4, make_green, 0)

        def weave(group, _):
            both = [
                gbuf[:, pl.ds(pl.multiple_of((2 * group + h) * 32, 32), 32), :].reshape(256, 128)
                for h in range(2)
            ]
            woven = dot(sw[...], jnp.concatenate(both, axis=1)).astype(BF)
            for h in range(2):
                piece = woven[:, 128 * h : 128 * (h + 1)].reshape(8, 32, 128)
                stage1[chunk, pl.ds((2 * group + h) * 8, 8)] = piece
            return 0

        lax.fori_loop(0, 8, weave, 0)

        def send(i, _):
            to = partner(i)
            pltpu.make_async_remote_copy(
                stage1.at[chunk, to[0] * 8 + to[1]],
                got1.at[chunk, me],
                send1.at[chunk],
                recv1.at[chunk],
                device_id=to,
                device_id_type=pl.DeviceIdType.MESH,
            ).start()
            return 0

        lax.fori_loop(1, 128, send, 0)
        got1[chunk, me] = stage1[chunk, me]
        return 0

    lax.fori_loop(0, CHUNKS, outward, 0)

    def make_gcol(pt, _):
        for part in range(2):
            gcol[pt, part] = dot(g[pt, part], cols[...]).astype(BF)
        return 0

    lax.fori_loop(0, 4, make_gcol, 0)
    for copy in late[1:]:
        copy.wait()

    some = pl.ds(0, 127)

    def convolve(chunk, _):
        pltpu.make_async_copy(stage1.at[chunk, some], got1.at[chunk, some], recv1.at[chunk]).wait()
        for pair in range(2):
            held = got1[chunk, :, 16 * pair : 16 * pair + 16, :].astype(F32)
            held = held.reshape(2, 8, 2, 4, 16, 128)
            plus = held[0] + held[1]
            minus = held[0] - held[1]
            parts = (
                plus[:, 0] + plus[:, 1],
                plus[:, 0] - plus[:, 1],
                minus[:, 0] + minus[:, 1],
                minus[:, 0] - minus[:, 1],
            )
            done = []
            for kind in range(4):
                x = parts[kind]
                x = jnp.concatenate(
                    [x[:, :, 0:8].reshape(256, 128), x[:, :, 8:16].reshape(256, 128)], axis=1
                ).astype(BF)
                y = dot(tf[kind], x)
                lanes = [
                    pl.ds(pl.multiple_of((2 * pair + h) * 512 + chunk * WIDE, WIDE), WIDE)
                    for h in range(2)
                ]
                wr = jnp.concatenate([w[kind, 0, :, at] for at in lanes], axis=1).astype(F32)
                wi = jnp.concatenate([w[kind, 1, :, at] for at in lanes], axis=1).astype(F32)
                yr, yi = y[:128], y[128:]
                z = jnp.concatenate([yr * wr - yi * wi, yr * wi + yi * wr], axis=0).astype(BF)
                done.append(dot(ti[kind], z))
            up, down = done[0] + done[1], done[2] + done[3]
            cross_up, cross_down = done[0] - done[1], done[2] - done[3]
            results = ((up + down, cross_up + cross_down), (up - down, cross_up - cross_down))
            for eh in range(2):
                for mh in range(2):
                    x = results[eh][mh]
                    x = jnp.concatenate(
                        [x[:, :128].reshape(8, 4, 8, 128), x[:, 128:].reshape(8, 4, 8, 128)], axis=2
                    ).astype(BF)
                    for low in range(8):
                        at = (8 * eh + low) * 8 + 4 * mh
                        stage2[chunk, at : at + 4, 16 * pair : 16 * pair + 16, :] = x[low]

        def send(i, _):
            to = partner(i)
            pltpu.make_async_remote_copy(
                stage2.at[chunk, to[0] * 8 + to[1]],
                got2.at[chunk, me],
                send2.at[chunk],
                recv2.at[chunk],
                device_id=to,
                device_id_type=pl.DeviceIdType.MESH,
            ).start()
            return 0

        lax.fori_loop(1, 128, send, 0)
        got2[chunk, me] = stage2[chunk, me]
        return 0

    lax.fori_loop(0, CHUNKS, convolve, 0)

    for half in range(2):

        def inward(chunk, _):
            here = pl.ds(pl.multiple_of(chunk * WIDE, WIDE), WIDE)
            pltpu.make_async_copy(stage2.at[chunk, some], got2.at[chunk, some], recv2.at[chunk]).wait()

            def unweave(group, _):
                both = [
                    got2[chunk, pl.ds((2 * group + h) * 8, 8)].reshape(256, 128) for h in range(2)
                ]
                parted = dot(sw[...], jnp.concatenate(both, axis=1)).astype(BF)
                for h in range(2):
                    at = pl.ds(pl.multiple_of((2 * group + h) * 32, 32), 32)
                    for part in range(2):
                        sig[:, at, part * 128 : part * 128 + 128] = parted[
                            :, 128 * h : 128 * (h + 1)
                        ].reshape(4, 2, 32, 128)[:, part]
                return 0

            lax.fori_loop(0, 8, unweave, 0)

            def make_first2(pt, _):
                a = dot(gcol[pt, 0], sig[pt])
                b = dot(gcol[pt, 1], sig[pt])
                first[pt, 0, :, here] = (a[:, :WIDE] - b[:, WIDE:]).astype(BF)
                first[pt, 1, :, here] = (a[:, WIDE:] + b[:, :WIDE]).astype(BF)
                return 0

            lax.fori_loop(0, 4, make_first2, 0)
            return 0

        lax.fori_loop(2 * half, 2 * half + 2, inward, 0)
        span = slice(256 * half, 256 * half + 256)

        def finish(pt, _):
            fr, fi = first[pt, 0, :, span], first[pt, 1, :, span]
            gr, gi = g[pt, 0, :, span], g[pt, 1, :, span]
            real = dot_t(fr, gr) + dot_t(fi, gi)
            imag = dot_t(fi, gr) - dot_t(fr, gi)
            if half == 0:
                acc[pt, 0] = real
                acc[pt, 1] = imag
            else:
                s[pt, 0] = (acc[pt, 0] + real).astype(BF)
                s[pt, 1] = (acc[pt, 1] + imag).astype(BF)
                pltpu.make_async_copy(s.at[pt], out.at[pt], out_sem.at[pt]).start()
            return 0

        lax.fori_loop(0, 4, finish, 0)

    for chunk in range(CHUNKS):
        pltpu.make_async_copy(stage1.at[chunk, some], got1.at[chunk, some], send1.at[chunk]).wait()
        pltpu.make_async_copy(stage2.at[chunk, some], got2.at[chunk, some], send2.at[chunk]).wait()
    for pt in range(4):
        pltpu.make_async_copy(s.at[pt], out.at[pt], out_sem.at[pt]).wait()


def local(green_ret, sigma_in, screened, block_of_slot):
    forth, back = transforms()
    weight = screened.reshape(16, 2, 8, 2, 2, 2048).transpose(1, 3, 4, 0, 2, 5).reshape(4, 2, 128, 2048)
    hbm = pl.BlockSpec(memory_space=pl.ANY)
    exchange = pltpu.VMEM((CHUNKS, 128, 32, 128), BF)
    result = pl.pallas_call(
        kernel,
        out_shape=jax.ShapeDtypeStruct((4, 2, 512, 512), BF),
        in_specs=[pl.BlockSpec(memory_space=pltpu.VMEM)] + [hbm] * 6,
        out_specs=hbm,
        scratch_shapes=[
            pltpu.VMEM((4, 2, 512, 512), BF),
            pltpu.VMEM((4, 2, 512, 512), BF),
            pltpu.VMEM((4, 2, 128, 2048), BF),
            pltpu.VMEM((4, 256, 256), BF),
            pltpu.VMEM((4, 256, 256), BF),
            pltpu.VMEM((256, 256), BF),
            pltpu.VMEM((512, 512), BF),
            pltpu.VMEM((512, 512), BF),
            pltpu.VMEM((4, 2, 512, 512), BF),
            pltpu.VMEM((8, 512, 128), BF),
            pltpu.VMEM((4, 2, 512, 512), BF),
            exchange,
            exchange,
            exchange,
            exchange,
            pltpu.VMEM((4, 512, 256), BF),
            pltpu.VMEM((4, 2, 512, 512), F32),
            pltpu.SemaphoreType.DMA((12,)),
            pltpu.SemaphoreType.DMA((CHUNKS,)),
            pltpu.SemaphoreType.DMA((CHUNKS,)),
            pltpu.SemaphoreType.DMA((CHUNKS,)),
            pltpu.SemaphoreType.DMA((CHUNKS,)),
            pltpu.SemaphoreType.DMA((4,)),
        ],
        compiler_params=pltpu.CompilerParams(
            collective_id=0, has_side_effects=True, vmem_limit_bytes=60 << 20
        ),
    )(
        block_of_slot.reshape(1, 128),
        green_ret.reshape(4, 2, 512, 512),
        sigma_in.reshape(4, 2, 512, 512),
        weight,
        forth,
        back,
        swapper(),
    )
    return result.reshape(2, 2, 2, 512, 512)


def solution(mesh):
    in_specs = (
        P("energy", "momentum", None, None, None),
        P("energy", "momentum", None, None, None),
        P(("energy", "momentum"), None, None, None, None),
        P(),
    )
    out_specs = P("energy", "momentum", None, None, None)
    return jax.shard_map(local, mesh=mesh, in_specs=in_specs, out_specs=out_specs, check_vma=False)
```

time: 392 us -> 142 us (0.36); the launches traced: 385 us -> 142 us
  local copies, waits for them, and re-layouts: 130 us -> 11 us
  matrix products: 96 us -> 0 us
  other arithmetic: 21.7 us -> 0 us
  Pallas kernels: 137 us -> 131 us
    dot_general x32 -> x0, matrix products: 96 us -> none  [the longest x8 32.9 us: along_momentum(): jnp.einsum('nk,mkp->mnp', table, values, precision=lax.Precision.HIGH)]
    another operation x7 -> x0, local copies, waits for them, and re-layouts: 57 us -> none  [the longest x4 28.9 us: convolve(): jnp.stack([final_real, final_imag], axis=2) * factor]
    reshape x7 -> x1, local copies, waits for them, and re-layouts: 50.4 us -> 6.5 us  [local(): screened.reshape(16, 2, 8, 2, 2, 2048).transpose(1, 3, 4, 0, 2, 5)]
    transpose x2 -> x0, other arithmetic: 21.3 us -> none  [the longest x1 10.9 us: local(): green.reshape(2, 2, 2, 128, 2048).transpose(0, 1, 3, 2, 4)]
    unnamed x33 -> x1, local copies, waits for them, and re-layouts: 13.6 us -> 4.47 us
    transpose x1 -> x0, local copies, waits for them, and re-layouts: 8.7 us -> none  [local(): gathered = arrived.transpose(2, 0, 3, 1, 4, 5).reshape(32, 16, 2, 2048)]
    pallas_call x4 -> x1, Pallas kernels: 137 us -> 131 us  [local(): pl.pallas_call(kernel, out_shape=jax.ShapeDtypeStruct((4, 2, 512, 512), B...]
where the time goes in v2:
time: 142 us
  Pallas kernels  131 us (92%)
  local copies, waits for them, and re-layouts  11 us (8%)
    pallas_call x1, Pallas kernels, local(): pl.pallas_call(kernel, out_shape=jax.ShapeDtypeStruct((4, 2, 512, 512), B...  131 us
    reshape x1, local copies, waits for them, and re-layouts, local(): screened.reshape(16, 2, 8, 2, 2, 2048).transpose(1, 3, 4, 0, 2, 5)  6.5 us
    unnamed x1, local copies, waits for them, and re-layouts  4.47 us

profile of v2, /device:TPU:1, one launch (start us, length us, event | category | flops | bytes accessed | tf_op | source)
XLA Modules:
  0.0 141.9 jit_solution(10827365629405659045)
XLA Ops:
  0.0 6.5 %copy.8 = bf16[16,2,8,2,2,2048]{5,2,0,4,3,1:T(8,128)(2,1)} copy(bf16[16,2,8,2,2,2048]{5,4,3,2,1,0:T(2,128)(2,1)} %bitcast.10) | data formatting | bytes 8388608 | tf_op jit(solution)/shard_map/reshape | solution.py:293
  6.5 130.9 %shard_map.73 = bf16[4,2,512,512]{3,2,1,0:T(8,128)(2,1)} custom-call(s32[1,128]{1,0:T(1,128)} %bitcast.13, bf16[4,2,512,512]{3,2,1,0:T(8,128)(2,1)} %bitcast.11, bf16[4,2,512,512]{3,2,1,0:T(8,128)(2,1)} %bitcast.12, bf16[4,2,128,2048]{3,2,1,0:T(8,128)(2,1)} %bitcast.9, bf16[4,256,256]{2,1,0:T(8,128)(2,1)} %constant.6.clone.forth, ...), custom_call_target="tpu_custom_call" | custom-call | tf_op jit(solution)/shard_map/pallas_call | solution.py:296
  137.5 4.5 %copy.10 = bf16[2,2,2,512,512]{4,3,2,1,0:T(8,128)(2,1)} copy(bf16[2,2,2,512,512]{4,3,2,1,0:T(8,128)(2,1)} %bitcast.8) | data formatting | bytes 8388608

commit v3 on v2

v3 whole, which is shorter than its diff:
```python
import jax
import jax.numpy as jnp
import numpy as np
from jax import lax
from jax.experimental import pallas as pl
from jax.experimental.pallas import tpu as pltpu
from jax.sharding import PartitionSpec as P

BF = jnp.bfloat16
F32 = jnp.float32
CHUNKS = 4
WIDE = 128


def transforms():
    m, n = np.arange(16), np.arange(8)
    e, k = np.arange(16), np.arange(8)
    out = np.zeros((4, 256, 256), np.float64)
    for a in range(2):
        for b in range(2):
            steps = ((2 * m + a)[:, None, None, None] * e[None, None, :, None]) * 1.0 / 32
            steps = steps + ((2 * n + b)[None, :, None, None] * k[None, None, None, :]) * 1.0 / 16
            cos, sin = np.cos(2 * np.pi * steps), np.sin(2 * np.pi * steps)
            cols = np.zeros((2, 16, 8, 16, 8, 2))
            cols[0, ..., 0], cols[0, ..., 1] = cos, sin
            cols[1, ..., 0], cols[1, ..., 1] = -sin, cos
            cols = cols.reshape(2, 16, 8, 8, 2, 4, 2, 2).transpose(0, 1, 2, 3, 5, 4, 6, 7)
            out[2 * a + b] = cols.reshape(256, 256)
    back = out.transpose(0, 2, 1) / 512
    return jnp.asarray(out, BF), jnp.asarray(back, BF)


def weaver():
    row = np.arange(256)
    taken = (row % 8) * 32 + row // 8
    return np.arange(256)[None, :] == taken[:, None]


def splitter():
    row = np.arange(256)
    kind, part, m, n = row // 64, row // 32 % 2, row // 8 % 4, row % 8
    taken = ((2 * m + kind // 2) * 16 + 2 * n + kind % 2) * 2 + part
    return np.arange(256)[None, :] == taken[:, None]


def orders():
    return jnp.asarray(np.stack([weaver(), weaver().T, splitter()]), BF)


def dot(a, b):
    return jnp.dot(a, b, preferred_element_type=F32)


def dot_t(a, b):
    return lax.dot_general(a, b, (((1,), (1,)), ((), ())), preferred_element_type=F32)


def beside(a, b):
    return jnp.concatenate([a, b], axis=1)


def above(a, b):
    return jnp.concatenate([a, b], axis=0)


def kernel(
    order, order_row, green, sigma, screened, forth, back, moves, out,
    g, s, raw, w, tf, ti, mv, cols, first, gbuf, woven, gcol, stage1, got1, stage2, got2, sig, acc,
    load_sem, send1, recv1, send2, recv2, out_sem,
):
    e = lax.axis_index("energy")
    m = lax.axis_index("momentum")
    me = e * 8 + m
    my_z, my_y, my_x, my_core = e // 4, (m // 4) * 2 + (e // 2) % 2, m % 4, e % 2
    ys = [(my_y + i) % 4 for i in range(4)]
    zs = [(my_z + i) % 4 for i in range(4)]
    near = []
    for y in range(4):
        for z in range(4):
            for core in range(2):
                to_core = my_core if core == 0 else 1 - my_core
                near.append((zs[z] * 4 + (ys[y] % 2) * 2 + to_core, (ys[y] // 2) * 4))

    def each_partner(act):
        def at_x(x, _):
            xs = [(my_x + x + i) % 4 for i in range(4)]
            for k in range(32):
                to = (near[k][0], near[k][1] + xs[(k // 8 + k // 2) % 4])
                if k == 0:
                    pl.when(x > 0)(lambda to=to: act(to))
                else:
                    act(to)
            return 0

        lax.fori_loop(0, 4, at_x, 0)

    def load_point(pt):
        return (
            pltpu.make_async_copy(green.at[pt], g.at[pt], load_sem.at[pt]),
            pltpu.make_async_copy(sigma.at[pt], s.at[pt], load_sem.at[4 + pt]),
        )

    late = (
        pltpu.make_async_copy(moves, mv, load_sem.at[8]),
        pltpu.make_async_copy(forth, tf, load_sem.at[9]),
        pltpu.make_async_copy(back, ti, load_sem.at[10]),
    )
    for pt in range(4):
        for copy in load_point(pt):
            copy.start()
    for copy in late:
        copy.start()

    barrier = pltpu.get_barrier_semaphore()
    each_partner(
        lambda to: pl.semaphore_signal(
            barrier, inc=1, device_id=to, device_id_type=pl.DeviceIdType.MESH
        )
    )

    def make_first(pt, _):
        for copy in load_point(pt):
            copy.wait()
        sr, si = s[pt, 0], s[pt, 1]
        first[pt] = dot(beside(g[pt, 0], g[pt, 1]), above(beside(sr, si), beside(-si, sr))).astype(BF)
        return 0

    lax.fori_loop(0, 4, make_first, 0)
    late[0].wait()
    pl.semaphore_wait(barrier, 127)

    def outward(chunk, _):
        here = pl.ds(pl.multiple_of(chunk * WIDE, WIDE), WIDE)

        def make_green(pt, _):
            gr, gi = g[pt, 0, here, :], g[pt, 1, here, :]
            both = dot_t(first[pt], above(beside(gr, gi), beside(-gi, gr))).astype(BF)
            gbuf[2 * pt] = both[:, :WIDE]
            gbuf[2 * pt + 1] = both[:, WIDE:]
            return 0

        lax.fori_loop(0, 4, make_green, 0)

        def weave(group, _):
            both = [
                gbuf[:, pl.ds(pl.multiple_of((2 * group + h) * 32, 32), 32), :].reshape(256, 128)
                for h in range(2)
            ]
            mixed = dot(mv[0], beside(*both)).astype(BF)
            for h in range(2):
                piece = mixed[:, 128 * h : 128 * (h + 1)].reshape(8, 32, 128)
                woven[pl.ds((2 * group + h) * 8, 8)] = piece
            return 0

        lax.fori_loop(0, 8, weave, 0)

        def send(to):
            slot = to[0] * 8 + to[1]
            stage1[chunk, slot] = woven[order[slot]]
            pltpu.make_async_remote_copy(
                stage1.at[chunk, slot],
                got1.at[chunk, me],
                send1.at[chunk],
                recv1.at[chunk],
                device_id=to,
                device_id_type=pl.DeviceIdType.MESH,
            ).start()

        each_partner(send)
        got1[chunk, me] = woven[order[me]]
        return 0

    lax.fori_loop(0, CHUNKS, outward, 0)

    lane = lax.broadcasted_iota(jnp.int32, (128, 512), 1)
    slot = lax.broadcasted_iota(jnp.int32, (128, 512), 0)
    spread = (slot == lane // 4).astype(F32).astype(BF)
    blocks = jnp.broadcast_to(order_row[...].astype(F32), (8, 128)).astype(BF)
    lane1 = lax.broadcasted_iota(jnp.int32, (1, 512), 1)
    target = dot(blocks, spread)[0:1] * 4.0 + (lane1 % 4).astype(F32)
    index = lax.broadcasted_iota(jnp.int32, (512, 512), 0).astype(F32)
    cols[...] = jnp.where(index == target, 1.0, 0.0).astype(BF)

    def make_gcol(pt, _):
        for part in range(2):
            gcol[pt, :, 512 * part : 512 * part + 512] = dot(g[pt, part], cols[...]).astype(BF)
        return 0

    lax.fori_loop(0, 4, make_gcol, 0)

    def split(group, _):
        load = pltpu.make_async_copy(screened.at[pl.ds(group * 8, 8)], raw, load_sem.at[11])
        load.start()
        load.wait()
        parted = dot(mv[2], raw[...].reshape(256, 2048)).astype(BF)
        w[:, :, pl.ds(pl.multiple_of(group * 32, 32), 32), :] = parted.reshape(4, 2, 32, 2048)
        return 0

    lax.fori_loop(0, 4, split, 0)
    for copy in late[1:]:
        copy.wait()

    some = pl.ds(0, 127)

    def convolve(chunk, _):
        pltpu.make_async_copy(stage1.at[chunk, some], got1.at[chunk, some], recv1.at[chunk]).wait()
        for pair in range(2):
            held = got1[chunk, :, 16 * pair : 16 * pair + 16, :].astype(F32)
            held = held.reshape(2, 8, 2, 4, 16, 128)
            plus = held[0] + held[1]
            minus = held[0] - held[1]
            parts = (
                plus[:, 0] + plus[:, 1],
                plus[:, 0] - plus[:, 1],
                minus[:, 0] + minus[:, 1],
                minus[:, 0] - minus[:, 1],
            )
            done = []
            for kind in range(4):
                x = parts[kind]
                x = beside(x[:, :, 0:8].reshape(256, 128), x[:, :, 8:16].reshape(256, 128))
                y = dot(tf[kind], x.astype(BF))
                lanes = [
                    pl.ds(pl.multiple_of((2 * pair + h) * 512 + chunk * WIDE, WIDE), WIDE)
                    for h in range(2)
                ]
                wr = beside(*[w[kind, 0, :, at] for at in lanes]).astype(F32)
                wi = beside(*[w[kind, 1, :, at] for at in lanes]).astype(F32)
                yr, yi = y[:128], y[128:]
                z = above(yr * wr - yi * wi, yr * wi + yi * wr).astype(BF)
                done.append(dot(ti[kind], z))
            up, down = done[0] + done[1], done[2] + done[3]
            cross_up, cross_down = done[0] - done[1], done[2] - done[3]
            results = ((up + down, cross_up + cross_down), (up - down, cross_up - cross_down))
            for eh in range(2):
                for mh in range(2):
                    x = results[eh][mh]
                    x = jnp.concatenate(
                        [x[:, :128].reshape(8, 4, 8, 128), x[:, 128:].reshape(8, 4, 8, 128)], axis=2
                    ).astype(BF)
                    for low in range(8):
                        at = (8 * eh + low) * 8 + 4 * mh
                        stage2[chunk, at : at + 4, 16 * pair : 16 * pair + 16, :] = x[low]

        def send(to):
            pltpu.make_async_remote_copy(
                stage2.at[chunk, to[0] * 8 + to[1]],
                got2.at[chunk, me],
                send2.at[chunk],
                recv2.at[chunk],
                device_id=to,
                device_id_type=pl.DeviceIdType.MESH,
            ).start()

        each_partner(send)
        got2[chunk, me] = stage2[chunk, me]
        return 0

    lax.fori_loop(0, CHUNKS, convolve, 0)

    for chunk in range(CHUNKS):
        span = slice(WIDE * chunk, WIDE * chunk + WIDE)
        pltpu.make_async_copy(stage2.at[chunk, some], got2.at[chunk, some], recv2.at[chunk]).wait()

        def unweave(group, _):
            both = [got2[chunk, pl.ds((2 * group + h) * 8, 8)].reshape(256, 128) for h in range(2)]
            parted = dot(mv[1], beside(*both)).astype(BF)
            for h in range(2):
                at = pl.ds(pl.multiple_of((2 * group + h) * 32, 32), 32)
                piece = parted[:, 128 * h : 128 * (h + 1)].reshape(4, 2, 32, 128)
                sig[:, 0, at, :] = piece[:, 0]
                sig[:, 1, at, :] = piece[:, 1]
            return 0

        lax.fori_loop(0, 8, unweave, 0)

        def inward(pt, _):
            sr, si = sig[pt, 0], sig[pt, 1]
            mine = dot(gcol[pt], above(beside(sr, si), beside(-si, sr))).astype(BF)
            gr, gi = g[pt, 0, :, span], g[pt, 1, :, span]
            part = dot_t(mine, above(beside(gr, gi), beside(-gi, gr)))
            if chunk > 0:
                part = part + acc[pt]
            if chunk < CHUNKS - 1:
                acc[pt] = part
            else:
                part = part.astype(BF)
                s[pt, 0] = part[:, :512]
                s[pt, 1] = part[:, 512:]
                pltpu.make_async_copy(s.at[pt], out.at[pt], out_sem.at[pt]).start()
            return 0

        lax.fori_loop(0, 4, inward, 0)

    for chunk in range(CHUNKS):
        pltpu.make_async_copy(stage1.at[chunk, some], got1.at[chunk, some], send1.at[chunk]).wait()
        pltpu.make_async_copy(stage2.at[chunk, some], got2.at[chunk, some], send2.at[chunk]).wait()
    for pt in range(4):
        pltpu.make_async_copy(s.at[pt], out.at[pt], out_sem.at[pt]).wait()


def local(green_ret, sigma_in, screened, block_of_slot):
    forth, back = transforms()
    hbm = pl.BlockSpec(memory_space=pl.ANY)
    exchange = pltpu.VMEM((CHUNKS, 128, 32, 128), BF)
    result = pl.pallas_call(
        kernel,
        out_shape=jax.ShapeDtypeStruct((4, 2, 512, 512), BF),
        in_specs=[pl.BlockSpec(memory_space=pltpu.SMEM), pl.BlockSpec(memory_space=pltpu.VMEM)]
        + [hbm] * 6,
        out_specs=hbm,
        scratch_shapes=[
            pltpu.VMEM((4, 2, 512, 512), BF),
            pltpu.VMEM((4, 2, 512, 512), BF),
            pltpu.VMEM((8, 16, 2, 2048), BF),
            pltpu.VMEM((4, 2, 128, 2048), BF),
            pltpu.VMEM((4, 256, 256), BF),
            pltpu.VMEM((4, 256, 256), BF),
            pltpu.VMEM((3, 256, 256), BF),
            pltpu.VMEM((512, 512), BF),
            pltpu.VMEM((4, 512, 1024), BF),
            pltpu.VMEM((8, 512, 128), BF),
            pltpu.VMEM((128, 32, 128), BF),
            pltpu.VMEM((4, 512, 1024), BF),
            exchange,
            exchange,
            exchange,
            exchange,
            pltpu.VMEM((4, 2, 512, 128), BF),
            pltpu.VMEM((4, 512, 1024), F32),
            pltpu.SemaphoreType.DMA((12,)),
            pltpu.SemaphoreType.DMA((CHUNKS,)),
            pltpu.SemaphoreType.DMA((CHUNKS,)),
            pltpu.SemaphoreType.DMA((CHUNKS,)),
            pltpu.SemaphoreType.DMA((CHUNKS,)),
            pltpu.SemaphoreType.DMA((4,)),
        ],
        compiler_params=pltpu.CompilerParams(
            collective_id=0, has_side_effects=True, vmem_limit_bytes=56 << 20
        ),
    )(
        block_of_slot,
        block_of_slot.reshape(1, 128),
        green_ret.reshape(4, 2, 512, 512),
        sigma_in.reshape(4, 2, 512, 512),
        screened.reshape(32, 16, 2, 2048),
        forth,
        back,
        orders(),
    )
    return result.reshape(2, 2, 2, 512, 512)


def solution(mesh):
    in_specs = (
        P("energy", "momentum", None, None, None),
        P("energy", "momentum", None, None, None),
        P(("energy", "momentum"), None, None, None, None),
        P(),
    )
    out_specs = P("energy", "momentum", None, None, None)
    return jax.shard_map(local, mesh=mesh, in_specs=in_specs, out_specs=out_specs, check_vma=False)
```

time: 142 us -> 124 us (0.87)
  Pallas kernels: 131 us -> 119 us
  local copies, waits for them, and re-layouts: 11 us -> 4.47 us
    pallas_call x1, Pallas kernels: 131 us -> 119 us  [local(): pl.pallas_call(kernel, out_shape=jax.ShapeDtypeStruct((4, 2, 512, 512), B...]
    reshape x1 -> x0, local copies, waits for them, and re-layouts: 6.5 us -> none  [local(): screened.reshape(16, 2, 8, 2, 2, 2048).transpose(1, 3, 4, 0, 2, 5)]
where the time goes in v3:
time: 124 us; the launch traced here: 123 us
  Pallas kernels  119 us (96%)
  local copies, waits for them, and re-layouts  4.47 us (4%)
    pallas_call x1, Pallas kernels, local(): pl.pallas_call(kernel, out_shape=jax.ShapeDtypeStruct((4, 2, 512, 512), B...  119 us
    unnamed x1, local copies, waits for them, and re-layouts  4.47 us

profile of v3, /device:TPU:1, one launch (start us, length us, event | category | flops | bytes accessed | tf_op | source)
XLA Modules:
  0.0 123.4 jit_solution(1152835478587847547)
XLA Ops:
  0.0 118.9 %shard_map.73 = bf16[4,2,512,512]{3,2,1,0:T(8,128)(2,1)} custom-call(s32[128]{0:T(128)} %order.1, s32[1,128]{1,0:T(1,128)} %bitcast.9, bf16[4,2,512,512]{3,2,1,0:T(8,128)(2,1)} %bitcast.6, bf16[4,2,512,512]{3,2,1,0:T(8,128)(2,1)} %bitcast.7, bf16[32,16,2,2048]{3,2,1,0:T(2,128)(2,1)} %bitcast.8, bf16[4,256,256]{2,1,0:T(8,128)(2,1)} %constant.6.clone.forth, ...), custom_call_target="tpu_custom_call" | custom-call | tf_op jit(solution)/shard_map/pallas_call | solution.py:306
  118.9 4.5 %copy.9 = bf16[2,2,2,512,512]{4,3,2,1,0:T(8,128)(2,1)} copy(bf16[2,2,2,512,512]{4,3,2,1,0:T(8,128)(2,1)} %bitcast.5) | data formatting | bytes 8388608

commit v4 on v3

--- a/solution.py
+++ b/solution.py
@@ -26,8 +26,7 @@
             cols[1, ..., 0], cols[1, ..., 1] = -sin, cos
             cols = cols.reshape(2, 16, 8, 8, 2, 4, 2, 2).transpose(0, 1, 2, 3, 5, 4, 6, 7)
             out[2 * a + b] = cols.reshape(256, 256)
-    back = out.transpose(0, 2, 1) / 512
-    return jnp.asarray(out, BF), jnp.asarray(back, BF)
+    return out
 
 
 def weaver():
@@ -43,8 +42,27 @@
     return np.arange(256)[None, :] == taken[:, None]
 
 
-def orders():
-    return jnp.asarray(np.stack([weaver(), weaver().T, splitter()]), BF)
+def half_weaver():
+    row = np.arange(256)
+    taken = (row % 4) * 64 + row // 4
+    return np.arange(256)[None, :] == taken[:, None]
+
+
+def joiner():
+    row = np.arange(256)
+    taken = (row // 4 % 2) * 128 + (row // 32) * 16 + (row // 8 % 4) * 4 + row % 4
+    return np.arange(256)[None, :] == taken[:, None]
+
+
+FORTH, BACK, WEAVE, UNWEAVE, SPLIT, HALF_WEAVE, HALF_UNWEAVE, JOIN, PART = 0, 4, 8, 9, 10, 11, 12, 13, 14
+MATRICES, ROOM = 15, 40
+
+
+def matrices():
+    forth = transforms()
+    moves = [weaver(), weaver().T, splitter(), half_weaver(), half_weaver().T, joiner(), joiner().T]
+    spare = np.zeros((ROOM - MATRICES, 256, 256))
+    return jnp.asarray(np.concatenate([forth, forth.transpose(0, 2, 1) / 512, np.stack(moves), spare]), BF)
 
 
 def dot(a, b):
@@ -64,9 +82,9 @@
 
 
 def kernel(
-    order, order_row, green, sigma, screened, forth, back, moves, out,
-    g, s, raw, w, tf, ti, mv, cols, first, gbuf, woven, gcol, stage1, got1, stage2, got2, sig, acc,
-    load_sem, send1, recv1, send2, recv2, out_sem,
+    order, order_row, green, sigma, screened, tables, out,
+    g, s, raw, mv, cols, first, gbuf, woven, half_woven, stage, got1, got2, sig, acc,
+    half_stage, half_got, last_got, load_sem, send1, recv1, send2, recv2, half_sem, out_sem,
 ):
     e = lax.axis_index("energy")
     m = lax.axis_index("momentum")
@@ -100,16 +118,11 @@
             pltpu.make_async_copy(sigma.at[pt], s.at[pt], load_sem.at[4 + pt]),
         )
 
-    late = (
-        pltpu.make_async_copy(moves, mv, load_sem.at[8]),
-        pltpu.make_async_copy(forth, tf, load_sem.at[9]),
-        pltpu.make_async_copy(back, ti, load_sem.at[10]),
-    )
+    late = pltpu.make_async_copy(tables.at[pl.ds(0, MATRICES)], mv, load_sem.at[8])
     for pt in range(4):
         for copy in load_point(pt):
             copy.start()
-    for copy in late:
-        copy.start()
+    late.start()
 
     barrier = pltpu.get_barrier_semaphore()
     each_partner(
@@ -125,11 +138,7 @@
         first[pt] = dot(beside(g[pt, 0], g[pt, 1]), above(beside(sr, si), beside(-si, sr))).astype(BF)
         return 0
 
-    lax.fori_loop(0, 4, make_first, 0)
-    late[0].wait()
-    pl.semaphore_wait(barrier, 127)
-
-    def outward(chunk, _):
+    def green_of(chunk):
         here = pl.ds(pl.multiple_of(chunk * WIDE, WIDE), WIDE)
 
         def make_green(pt, _):
@@ -139,14 +148,55 @@
             gbuf[2 * pt + 1] = both[:, WIDE:]
             return 0
 
-        lax.fori_loop(0, 4, make_green, 0)
+        return make_green
+
+    for half in range(2):
+        lax.fori_loop(2 * half, 2 * half + 2, make_first, 0)
+        lax.fori_loop(2 * half, 2 * half + 2, green_of(0), 0)
+        if half == 0:
+            late.wait()
+
+        def half_weave(group, _):
+            both = [
+                gbuf[
+                    4 * half : 4 * half + 4, pl.ds(pl.multiple_of((2 * group + h) * 64, 64), 64), :
+                ].reshape(256, 128)
+                for h in range(2)
+            ]
+            mixed = dot(mv[HALF_WEAVE], beside(*both)).astype(BF)
+            for h in range(2):
+                piece = mixed[:, 128 * h : 128 * (h + 1)].reshape(16, 16, 128)
+                half_woven[pl.ds((2 * group + h) * 16, 16)] = piece
+            return 0
+
+        lax.fori_loop(0, 4, half_weave, 0)
+        if half == 0:
+            pl.semaphore_wait(barrier, 127)
+
+        def send_half(to):
+            slot = to[0] * 8 + to[1]
+            half_stage[half, slot] = half_woven[order[slot]]
+            pltpu.make_async_remote_copy(
+                half_stage.at[half, slot],
+                half_got.at[half, me],
+                half_sem.at[half],
+                half_sem.at[2 + half],
+                device_id=to,
+                device_id_type=pl.DeviceIdType.MESH,
+            ).start()
+
+        each_partner(send_half)
+        half_got[half, me] = half_woven[order[me]]
+
+    def outward(chunk, _):
+        lax.fori_loop(0, 4, green_of(chunk), 0)
 
         def weave(group, _):
             both = [
                 gbuf[:, pl.ds(pl.multiple_of((2 * group + h) * 32, 32), 32), :].reshape(256, 128)
                 for h in range(2)
             ]
-            mixed = dot(mv[0], beside(*both)).astype(BF)
+            mixed = dot(mv[WEAVE], beside(*both)).astype(BF)
             for h in range(2):
                 piece = mixed[:, 128 * h : 128 * (h + 1)].reshape(8, 32, 128)
                 woven[pl.ds((2 * group + h) * 8, 8)] = piece
@@ -156,9 +206,9 @@
 
         def send(to):
             slot = to[0] * 8 + to[1]
-            stage1[chunk, slot] = woven[order[slot]]
+            stage[chunk, slot] = woven[order[slot]]
             pltpu.make_async_remote_copy(
-                stage1.at[chunk, slot],
+                stage.at[chunk, slot],
                 got1.at[chunk, me],
                 send1.at[chunk],
                 recv1.at[chunk],
@@ -170,7 +220,7 @@
         got1[chunk, me] = woven[order[me]]
         return 0
 
-    lax.fori_loop(0, CHUNKS, outward, 0)
+    lax.fori_loop(1, CHUNKS, outward, 0)
 
     lane = lax.broadcasted_iota(jnp.int32, (128, 512), 1)
     slot = lax.broadcasted_iota(jnp.int32, (128, 512), 0)
@@ -183,7 +233,7 @@
 
     def make_gcol(pt, _):
         for part in range(2):
-            gcol[pt, :, 512 * part : 512 * part + 512] = dot(g[pt, part], cols[...]).astype(BF)
+            first[pt, :, 512 * part : 512 * part + 512] = dot(g[pt, part], cols[...]).astype(BF)
         return 0
 
     lax.fori_loop(0, 4, make_gcol, 0)
@@ -192,18 +242,45 @@
         load = pltpu.make_async_copy(screened.at[pl.ds(group * 8, 8)], raw, load_sem.at[11])
         load.start()
         load.wait()
-        parted = dot(mv[2], raw[...].reshape(256, 2048)).astype(BF)
-        w[:, :, pl.ds(pl.multiple_of(group * 32, 32), 32), :] = parted.reshape(4, 2, 32, 2048)
+        parted = dot(mv[SPLIT], raw[...].reshape(256, 2048)).astype(BF)
+        for row in range(4):
+            at = pl.ds(pl.multiple_of(row * 128 + group * 32, 32), 32)
+            s[:, :, at, :] = parted[:, 512 * row : 512 * row + 512].reshape(4, 2, 32, 512)
         return 0
 
     lax.fori_loop(0, 4, split, 0)
-    for copy in late[1:]:
-        copy.wait()
 
     some = pl.ds(0, 127)
 
+    def whole(half, sem):
+        return pltpu.make_async_copy(
+            half_stage.at[half, some], half_got.at[half, some], half_sem.at[sem + half]
+        )
+
+    for half in range(2):
+        whole(half, 2).wait()
+
+    def join(group, _):
+        both = [
+            half_got[:, pl.ds((2 * group + h) * 8, 8)].reshape(256, 128) for h in range(2)
+        ]
+        mixed = dot(mv[JOIN], beside(*both)).astype(BF)
+        for h in range(2):
+            piece = mixed[:, 128 * h : 128 * (h + 1)].reshape(8, 32, 128)
+            got1[0, pl.ds((2 * group + h) * 8, 8)] = piece
+        return 0
+
+    lax.fori_loop(0, 8, join, 0)
+    for half in range(2):
+        whole(half, 0).wait()
+
     def convolve(chunk, _):
-        pltpu.make_async_copy(stage1.at[chunk, some], got1.at[chunk, some], recv1.at[chunk]).wait()
+        @pl.when(chunk > 0)
+        def _():
+            pltpu.make_async_copy(stage.at[chunk, some], got1.at[chunk, some], recv1.at[chunk]).wait()
+            pltpu.make_async_copy(stage.at[chunk, some], got1.at[chunk, some], send1.at[chunk]).wait()
+
+        here = pl.ds(pl.multiple_of(chunk * WIDE, WIDE), WIDE)
         for pair in range(2):
             held = got1[chunk, :, 16 * pair : 16 * pair + 16, :].astype(F32)
             held = held.reshape(2, 8, 2, 4, 16, 128)
@@ -219,16 +296,13 @@
             for kind in range(4):
                 x = parts[kind]
                 x = beside(x[:, :, 0:8].reshape(256, 128), x[:, :, 8:16].reshape(256, 128))
-                y = dot(tf[kind], x.astype(BF))
-                lanes = [
-                    pl.ds(pl.multiple_of((2 * pair + h) * 512 + chunk * WIDE, WIDE), WIDE)
-                    for h in range(2)
-                ]
-                wr = beside(*[w[kind, 0, :, at] for at in lanes]).astype(F32)
-                wi = beside(*[w[kind, 1, :, at] for at in lanes]).astype(F32)
+                y = dot(mv[FORTH + kind], x.astype(BF))
+                spans = [pl.ds((2 * pair + h) * 128, 128) for h in range(2)]
+                wr = beside(*[s[kind, 0, at, here] for at in spans]).astype(F32)
+                wi = beside(*[s[kind, 1, at, here] for at in spans]).astype(F32)
                 yr, yi = y[:128], y[128:]
                 z = above(yr * wr - yi * wi, yr * wi + yi * wr).astype(BF)
-                done.append(dot(ti[kind], z))
+                done.append(dot(mv[BACK + kind], z))
             up, down = done[0] + done[1], done[2] + done[3]
             cross_up, cross_down = done[0] - done[1], done[2] - done[3]
             results = ((up + down, cross_up + cross_down), (up - down, cross_up - cross_down))
@@ -240,11 +314,11 @@
                     ).astype(BF)
                     for low in range(8):
                         at = (8 * eh + low) * 8 + 4 * mh
-                        stage2[chunk, at : at + 4, 16 * pair : 16 * pair + 16, :] = x[low]
+                        stage[chunk, at : at + 4, 16 * pair : 16 * pair + 16, :] = x[low]
 
         def send(to):
             pltpu.make_async_remote_copy(
-                stage2.at[chunk, to[0] * 8 + to[1]],
+                stage.at[chunk, to[0] * 8 + to[1]],
                 got2.at[chunk, me],
                 send2.at[chunk],
                 recv2.at[chunk],
@@ -252,19 +326,68 @@
                 device_id_type=pl.DeviceIdType.MESH,
             ).start()
 
-        each_partner(send)
-        got2[chunk, me] = stage2[chunk, me]
+        @pl.when(chunk < CHUNKS - 1)
+        def _():
+            each_partner(send)
+            got2[chunk, me] = stage[chunk, me]
+
         return 0
 
     lax.fori_loop(0, CHUNKS, convolve, 0)
 
-    for chunk in range(CHUNKS):
+    def part(group, _):
+        both = [
+            stage[CHUNKS - 1, pl.ds((2 * group + h) * 8, 8)].reshape(256, 128) for h in range(2)
+        ]
+        mixed = dot(mv[PART], beside(*both)).astype(BF)
+        for h in range(2):
+            piece = mixed[:, 128 * h : 128 * (h + 1)].reshape(2, 8, 16, 128)
+            half_stage[:, pl.ds((2 * group + h) * 8, 8)] = piece
+        return 0
+
+    lax.fori_loop(0, 8, part, 0)
+    for half in range(2):
+
+        def send_last(to):
+            pltpu.make_async_remote_copy(
+                half_stage.at[half, to[0] * 8 + to[1]],
+                last_got.at[half, me],
+                half_sem.at[4 + half],
+                half_sem.at[6 + half],
+                device_id=to,
+                device_id_type=pl.DeviceIdType.MESH,
+            ).start()
+
+        each_partner(send_last)
+        last_got[half, me] = half_stage[half, me]
+
+    def inward(chunk):
         span = slice(WIDE * chunk, WIDE * chunk + WIDE)
-        pltpu.make_async_copy(stage2.at[chunk, some], got2.at[chunk, some], recv2.at[chunk]).wait()
+
+        def at_point(pt, _):
+            sr, si = sig[pt, 0], sig[pt, 1]
+            mine = dot(first[pt], above(beside(sr, si), beside(-si, sr))).astype(BF)
+            gr, gi = g[pt, 0, :, span], g[pt, 1, :, span]
+            total = dot_t(mine, above(beside(gr, gi), beside(-gi, gr)))
+            if chunk > 0:
+                total = total + acc[pt]
+            if chunk < CHUNKS - 1:
+                acc[pt] = total
+            else:
+                total = total.astype(BF)
+                s[pt, 0] = total[:, :512]
+                s[pt, 1] = total[:, 512:]
+                pltpu.make_async_copy(s.at[pt], out.at[pt], out_sem.at[pt]).start()
+            return 0
+
+        return at_point
+
+    for chunk in range(CHUNKS - 1):
+        pltpu.make_async_copy(stage.at[chunk, some], got2.at[chunk, some], recv2.at[chunk]).wait()
 
         def unweave(group, _):
             both = [got2[chunk, pl.ds((2 * group + h) * 8, 8)].reshape(256, 128) for h in range(2)]
-            parted = dot(mv[1], beside(*both)).astype(BF)
+            parted = dot(mv[UNWEAVE], beside(*both)).astype(BF)
             for h in range(2):
                 at = pl.ds(pl.multiple_of((2 * group + h) * 32, 32), 32)
                 piece = parted[:, 128 * h : 128 * (h + 1)].reshape(4, 2, 32, 128)
@@ -273,70 +396,71 @@
             return 0
 
         lax.fori_loop(0, 8, unweave, 0)
-
-        def inward(pt, _):
-            sr, si = sig[pt, 0], sig[pt, 1]
-            mine = dot(gcol[pt], above(beside(sr, si), beside(-si, sr))).astype(BF)
-            gr, gi = g[pt, 0, :, span], g[pt, 1, :, span]
-            part = dot_t(mine, above(beside(gr, gi), beside(-gi, gr)))
-            if chunk > 0:
-                part = part + acc[pt]
-            if chunk < CHUNKS - 1:
-                acc[pt] = part
-            else:
-                part = part.astype(BF)
-                s[pt, 0] = part[:, :512]
-                s[pt, 1] = part[:, 512:]
-                pltpu.make_async_copy(s.at[pt], out.at[pt], out_sem.at[pt]).start()
-            return 0
-
-        lax.fori_loop(0, 4, inward, 0)
-
-    for chunk in range(CHUNKS):
-        pltpu.make_async_copy(stage1.at[chunk, some], got1.at[chunk, some], send1.at[chunk]).wait()
-        pltpu.make_async_copy(stage2.at[chunk, some], got2.at[chunk, some], send2.at[chunk]).wait()
+        lax.fori_loop(0, 4, inward(chunk), 0)
+
+    for half in range(2):
+        whole(half, 6).wait()
+
+        def half_unweave(group, _):
+            both = [
+                last_got[half, pl.ds((2 * group + h) * 16, 16)].reshape(256, 128) for h in range(2)
+            ]
+            parted = dot(mv[HALF_UNWEAVE], beside(*both)).astype(BF)
+            for h in range(2):
+                at = pl.ds(pl.multiple_of((2 * group + h) * 64, 64), 64)
+                piece = parted[:, 128 * h : 128 * (h + 1)].reshape(2, 2, 64, 128)
+                sig[2 * half : 2 * half + 2, :, at, :] = piece
+            return 0
+
+        lax.fori_loop(0, 4, half_unweave, 0)
+        lax.fori_loop(2 * half, 2 * half + 2, inward(CHUNKS - 1), 0)
+
+    for chunk in range(CHUNKS - 1):
+        pltpu.make_async_copy(stage.at[chunk, some], got2.at[chunk, some], send2.at[chunk]).wait()
+    for half in range(2):
+        whole(half, 4).wait()
     for pt in range(4):
         pltpu.make_async_copy(s.at[pt], out.at[pt], out_sem.at[pt]).wait()
 
 
 def local(green_ret, sigma_in, screened, block_of_slot):
-    forth, back = transforms()
-    hbm = pl.BlockSpec(memory_space=pl.ANY)
+    hbm = pl.BlockSpec(memory_space=pltpu.HBM)
     exchange = pltpu.VMEM((CHUNKS, 128, 32, 128), BF)
+    halves = pltpu.VMEM((2, 128, 16, 128), BF)
     result = pl.pallas_call(
         kernel,
         out_shape=jax.ShapeDtypeStruct((4, 2, 512, 512), BF),
         in_specs=[pl.BlockSpec(memory_space=pltpu.SMEM), pl.BlockSpec(memory_space=pltpu.VMEM)]
-        + [hbm] * 6,
-        out_specs=hbm,
+        + [hbm] * 4,
+        out_specs=pl.BlockSpec(memory_space=pl.ANY),
         scratch_shapes=[
             pltpu.VMEM((4, 2, 512, 512), BF),
             pltpu.VMEM((4, 2, 512, 512), BF),
             pltpu.VMEM((8, 16, 2, 2048), BF),
-            pltpu.VMEM((4, 2, 128, 2048), BF),
-            pltpu.VMEM((4, 256, 256), BF),
-            pltpu.VMEM((4, 256, 256), BF),
-            pltpu.VMEM((3, 256, 256), BF),
+            pltpu.VMEM((MATRICES, 256, 256), BF),
             pltpu.VMEM((512, 512), BF),
             pltpu.VMEM((4, 512, 1024), BF),
             pltpu.VMEM((8, 512, 128), BF),
             pltpu.VMEM((128, 32, 128), BF),
-            pltpu.VMEM((4, 512, 1024), BF),
-            exchange,
+            pltpu.VMEM((128, 16, 128), BF),
             exchange,
             exchange,
             exchange,
             pltpu.VMEM((4, 2, 512, 128), BF),
             pltpu.VMEM((4, 512, 1024), F32),
+            halves,
+            halves,
+            halves,
             pltpu.SemaphoreType.DMA((12,)),
             pltpu.SemaphoreType.DMA((CHUNKS,)),
             pltpu.SemaphoreType.DMA((CHUNKS,)),
             pltpu.SemaphoreType.DMA((CHUNKS,)),
             pltpu.SemaphoreType.DMA((CHUNKS,)),
+            pltpu.SemaphoreType.DMA((8,)),
             pltpu.SemaphoreType.DMA((4,)),
         ],
         compiler_params=pltpu.CompilerParams(
-            collective_id=0, has_side_effects=True, vmem_limit_bytes=56 << 20
+            collective_id=0, has_side_effects=True, vmem_limit_bytes=47 << 20
         ),
     )(
         block_of_slot,
@@ -344,9 +468,7 @@
         green_ret.reshape(4, 2, 512, 512),
         sigma_in.reshape(4, 2, 512, 512),
         screened.reshape(32, 16, 2, 2048),
-        forth,
-        back,
-        orders(),
+        matrices(),
     )
     return result.reshape(2, 2, 2, 512, 512)
 

time: 124 us -> 114 us (0.919)
  Pallas kernels: 119 us -> 111 us
  local copies, waits for them, and re-layouts: 4.47 us -> 2.67 us
    pallas_call x1, Pallas kernels: 119 us -> 111 us  [local(): pl.pallas_call(kernel, out_shape=jax.ShapeDtypeStruct((4, 2, 512, 512), B...]
    unnamed x1 -> x3, local copies, waits for them, and re-layouts: 4.47 us -> 2.67 us
where the time goes in v4:
time: 114 us; the launch traced here: 113 us
  Pallas kernels  111 us (97%)
  local copies, waits for them, and re-layouts  2.67 us (2%)
    pallas_call x1, Pallas kernels, local(): pl.pallas_call(kernel, out_shape=jax.ShapeDtypeStruct((4, 2, 512, 512), B...  111 us
    unnamed x3, local copies, waits for them, and re-layouts  2.67 us

profile of v4, /device:TPU:1, one launch (start us, length us, event | category | flops | bytes accessed | tf_op | source)
XLA Modules:
  0.0 113.4 jit_solution(8577680150362661627)
XLA Ops:
  0.0 0.0 copy-start
  0.0 0.7 copy-done
  0.7 110.8 %shard_map.55 = bf16[4,2,512,512]{3,2,1,0:T(8,128)(2,1)S(1)} custom-call(s32[128]{0:T(128)S(1)} %copy-done, s32[1,128]{1,0:T(1,128)S(1)} %bitcast.6, bf16[4,2,512,512]{3,2,1,0:T(8,128)(2,1)} %bitcast.7, bf16[4,2,512,512]{3,2,1,0:T(8,128)(2,1)} %bitcast.8, bf16[32,16,2,2048]{3,2,1,0:T(2,128)(2,1)} %bitcast.9, bf16[40,256,256]{2,1,0:T(8,128)(2,1)} %constant.2.clone.tables), custom_call_target="tpu_custom_call" | custom-call | tf_op jit(solution)/shard_map/pallas_call | solution.py:430
  111.4 2.0 %copy.7 = bf16[2,2,2,512,512]{4,3,2,1,0:T(8,128)(2,1)} copy(bf16[2,2,2,512,512]{4,3,2,1,0:T(8,128)(2,1)S(1)} %bitcast.5) | data formatting | bytes 8388608
Async XLA Ops:
  0.0 0.7 copy-start

commit v5 on v4

--- a/solution.py
+++ b/solution.py
@@ -50,7 +50,14 @@
 
 def joiner():
     row = np.arange(256)
-    taken = (row // 4 % 2) * 128 + (row // 32) * 16 + (row // 8 % 4) * 4 + row % 4
+    chunk, source, line, point, part = row // 128, row // 32 % 4, row // 8 % 4, row // 2 % 4, row % 2
+    taken = point * 64 + source * 16 + line * 4 + chunk * 2 + part
+    return np.arange(256)[None, :] == taken[:, None]
+
+
+def parter():
+    row = np.arange(256)
+    taken = (row // 16 % 8) * 32 + (row // 4 % 4) * 8 + (row // 128) * 4 + row % 4
     return np.arange(256)[None, :] == taken[:, None]
 
 
@@ -60,7 +67,7 @@
 
 def matrices():
     forth = transforms()
-    moves = [weaver(), weaver().T, splitter(), half_weaver(), half_weaver().T, joiner(), joiner().T]
+    moves = [weaver(), weaver().T, splitter(), half_weaver(), half_weaver().T, joiner(), parter()]
     spare = np.zeros((ROOM - MATRICES, 256, 256))
     return jnp.asarray(np.concatenate([forth, forth.transpose(0, 2, 1) / 512, np.stack(moves), spare]), BF)
 
@@ -150,17 +157,20 @@
 
         return make_green
 
-    for half in range(2):
-        lax.fori_loop(2 * half, 2 * half + 2, make_first, 0)
-        lax.fori_loop(2 * half, 2 * half + 2, green_of(0), 0)
-        if half == 0:
+    for pt in range(4):
+        make_first(pt, 0)
+        gr, gi = g[pt, 0, : 2 * WIDE, :], g[pt, 1, : 2 * WIDE, :]
+        early = dot_t(first[pt], above(beside(gr, gi), beside(-gi, gr))).astype(BF)
+        for chunk in range(2):
+            for part in range(2):
+                at = (2 * part + chunk) * WIDE
+                gbuf[2 * chunk + part] = early[:, at : at + WIDE]
+        if pt == 0:
             late.wait()
 
-        def half_weave(group, _):
+        def early_weave(group, _):
             both = [
-                gbuf[
-                    4 * half : 4 * half + 4, pl.ds(pl.multiple_of((2 * group + h) * 64, 64), 64), :
-                ].reshape(256, 128)
+                gbuf[0:4, pl.ds(pl.multiple_of((2 * group + h) * 64, 64), 64), :].reshape(256, 128)
                 for h in range(2)
             ]
             mixed = dot(mv[HALF_WEAVE], beside(*both)).astype(BF)
@@ -169,24 +179,24 @@
                 half_woven[pl.ds((2 * group + h) * 16, 16)] = piece
             return 0
 
-        lax.fori_loop(0, 4, half_weave, 0)
-        if half == 0:
+        lax.fori_loop(0, 4, early_weave, 0)
+        if pt == 0:
             pl.semaphore_wait(barrier, 127)
 
-        def send_half(to):
+        def send_early(to):
             slot = to[0] * 8 + to[1]
-            half_stage[half, slot] = half_woven[order[slot]]
+            half_stage[pt, slot] = half_woven[order[slot]]
             pltpu.make_async_remote_copy(
-                half_stage.at[half, slot],
-                half_got.at[half, me],
-                half_sem.at[half],
-                half_sem.at[2 + half],
+                half_stage.at[pt, slot],
+                half_got.at[pt, me],
+                half_sem.at[pt],
+                half_sem.at[4 + pt],
                 device_id=to,
                 device_id_type=pl.DeviceIdType.MESH,
             ).start()
 
-        each_partner(send_half)
-        half_got[half, me] = half_woven[order[me]]
+        each_partner(send_early)
+        half_got[pt, me] = half_woven[order[me]]
 
     def outward(chunk, _):
         lax.fori_loop(0, 4, green_of(chunk), 0)
@@ -220,7 +230,7 @@
         got1[chunk, me] = woven[order[me]]
         return 0
 
-    lax.fori_loop(1, CHUNKS, outward, 0)
+    lax.fori_loop(2, CHUNKS, outward, 0)
 
     lane = lax.broadcasted_iota(jnp.int32, (128, 512), 1)
     slot = lax.broadcasted_iota(jnp.int32, (128, 512), 0)
@@ -252,30 +262,28 @@
 
     some = pl.ds(0, 127)
 
-    def whole(half, sem):
+    def whole(piece, sem):
         return pltpu.make_async_copy(
-            half_stage.at[half, some], half_got.at[half, some], half_sem.at[sem + half]
+            half_stage.at[piece, some], half_got.at[piece, some], half_sem.at[sem + piece]
         )
 
-    for half in range(2):
-        whole(half, 2).wait()
+    for pt in range(4):
+        whole(pt, 4).wait()
 
     def join(group, _):
-        both = [
-            half_got[:, pl.ds((2 * group + h) * 8, 8)].reshape(256, 128) for h in range(2)
-        ]
+        both = [half_got[:, pl.ds((2 * group + h) * 4, 4)].reshape(256, 128) for h in range(2)]
         mixed = dot(mv[JOIN], beside(*both)).astype(BF)
         for h in range(2):
-            piece = mixed[:, 128 * h : 128 * (h + 1)].reshape(8, 32, 128)
-            got1[0, pl.ds((2 * group + h) * 8, 8)] = piece
-        return 0
-
-    lax.fori_loop(0, 8, join, 0)
-    for half in range(2):
-        whole(half, 0).wait()
+            piece = mixed[:, 128 * h : 128 * (h + 1)].reshape(2, 4, 32, 128)
+            got1[0:2, pl.ds((2 * group + h) * 4, 4)] = piece
+        return 0
+
+    lax.fori_loop(0, 16, join, 0)
+    for pt in range(4):
+        whole(pt, 0).wait()
 
     def convolve(chunk, _):
-        @pl.when(chunk > 0)
+        @pl.when(chunk > 1)
         def _():
             pltpu.make_async_copy(stage.at[chunk, some], got1.at[chunk, some], recv1.at[chunk]).wait()
             pltpu.make_async_copy(stage.at[chunk, some], got1.at[chunk, some], send1.at[chunk]).wait()
@@ -342,7 +350,7 @@
         mixed = dot(mv[PART], beside(*both)).astype(BF)
         for h in range(2):
             piece = mixed[:, 128 * h : 128 * (h + 1)].reshape(2, 8, 16, 128)
-            half_stage[:, pl.ds((2 * group + h) * 8, 8)] = piece
+            half_stage[0:2, pl.ds((2 * group + h) * 8, 8)] = piece
         return 0
 
     lax.fori_loop(0, 8, part, 0)
@@ -352,8 +360,8 @@
             pltpu.make_async_remote_copy(
                 half_stage.at[half, to[0] * 8 + to[1]],
                 last_got.at[half, me],
-                half_sem.at[4 + half],
-                half_sem.at[6 + half],
+                half_sem.at[8 + half],
+                half_sem.at[10 + half],
                 device_id=to,
                 device_id_type=pl.DeviceIdType.MESH,
             ).start()
@@ -399,7 +407,7 @@
         lax.fori_loop(0, 4, inward(chunk), 0)
 
     for half in range(2):
-        whole(half, 6).wait()
+        whole(half, 10).wait()
 
         def half_unweave(group, _):
             both = [
@@ -418,7 +426,7 @@
     for chunk in range(CHUNKS - 1):
         pltpu.make_async_copy(stage.at[chunk, some], got2.at[chunk, some], send2.at[chunk]).wait()
     for half in range(2):
-        whole(half, 4).wait()
+        whole(half, 8).wait()
     for pt in range(4):
         pltpu.make_async_copy(s.at[pt], out.at[pt], out_sem.at[pt]).wait()
 
@@ -426,7 +434,7 @@
 def local(green_ret, sigma_in, screened, block_of_slot):
     hbm = pl.BlockSpec(memory_space=pltpu.HBM)
     exchange = pltpu.VMEM((CHUNKS, 128, 32, 128), BF)
-    halves = pltpu.VMEM((2, 128, 16, 128), BF)
+    quarters = pltpu.VMEM((4, 128, 16, 128), BF)
     result = pl.pallas_call(
         kernel,
         out_shape=jax.ShapeDtypeStruct((4, 2, 512, 512), BF),
@@ -448,19 +456,19 @@
             exchange,
             pltpu.VMEM((4, 2, 512, 128), BF),
             pltpu.VMEM((4, 512, 1024), F32),
-            halves,
-            halves,
-            halves,
+            quarters,
+            quarters,
+            pltpu.VMEM((2, 128, 16, 128), BF),
             pltpu.SemaphoreType.DMA((12,)),
             pltpu.SemaphoreType.DMA((CHUNKS,)),
             pltpu.SemaphoreType.DMA((CHUNKS,)),
             pltpu.SemaphoreType.DMA((CHUNKS,)),
             pltpu.SemaphoreType.DMA((CHUNKS,)),
-            pltpu.SemaphoreType.DMA((8,)),
+            pltpu.SemaphoreType.DMA((12,)),
             pltpu.SemaphoreType.DMA((4,)),
         ],
         compiler_params=pltpu.CompilerParams(
-            collective_id=0, has_side_effects=True, vmem_limit_bytes=47 << 20
+            collective_id=0, has_side_effects=True, vmem_limit_bytes=48 << 20
         ),
     )(
         block_of_slot,

time: 114 us -> 113 us (level)
  no operation moved by 1% of the time
where the time goes in v5:
time: 113 us
  Pallas kernels  110 us (97%)
  local copies, waits for them, and re-layouts  2.67 us (2%)
    pallas_call x1, Pallas kernels, local(): pl.pallas_call(kernel, out_shape=jax.ShapeDtypeStruct((4, 2, 512, 512), B...  110 us
    unnamed x3, local copies, waits for them, and re-layouts  2.67 us

profile of v5, /device:TPU:1, one launch (start us, length us, event | category | flops | bytes accessed | tf_op | source)
XLA Modules:
  0.0 112.5 jit_solution(18101696921573128541)
XLA Ops:
  0.0 0.0 copy-start
  0.0 0.7 copy-done
  0.7 109.8 %shard_map.55 = bf16[4,2,512,512]{3,2,1,0:T(8,128)(2,1)S(1)} custom-call(s32[128]{0:T(128)S(1)} %copy-done, s32[1,128]{1,0:T(1,128)S(1)} %bitcast.6, bf16[4,2,512,512]{3,2,1,0:T(8,128)(2,1)} %bitcast.7, bf16[4,2,512,512]{3,2,1,0:T(8,128)(2,1)} %bitcast.8, bf16[32,16,2,2048]{3,2,1,0:T(2,128)(2,1)} %bitcast.9, bf16[40,256,256]{2,1,0:T(8,128)(2,1)} %constant.2.clone.tables), custom_call_target="tpu_custom_call" | custom-call | tf_op jit(solution)/shard_map/pallas_call | solution.py:438
  110.5 2.0 %copy.7 = bf16[2,2,2,512,512]{4,3,2,1,0:T(8,128)(2,1)} copy(bf16[2,2,2,512,512]{4,3,2,1,0:T(8,128)(2,1)S(1)} %bitcast.5) | data formatting | bytes 8388608
Async XLA Ops:
  0.0 0.7 copy-start

commit v6 on v5

--- a/solution.py
+++ b/solution.py
@@ -61,15 +61,15 @@
     return np.arange(256)[None, :] == taken[:, None]
 
 
-FORTH, BACK, WEAVE, UNWEAVE, SPLIT, HALF_WEAVE, HALF_UNWEAVE, JOIN, PART = 0, 4, 8, 9, 10, 11, 12, 13, 14
+HALF_WEAVE, FORTH, BACK, WEAVE, UNWEAVE, SPLIT, HALF_UNWEAVE, JOIN, PART = 0, 1, 5, 9, 10, 11, 12, 13, 14
 MATRICES, ROOM = 15, 40
 
 
 def matrices():
     forth = transforms()
-    moves = [weaver(), weaver().T, splitter(), half_weaver(), half_weaver().T, joiner(), parter()]
+    moves = [weaver(), weaver().T, splitter(), half_weaver().T, joiner(), parter()]
     spare = np.zeros((ROOM - MATRICES, 256, 256))
-    return jnp.asarray(np.concatenate([forth, forth.transpose(0, 2, 1) / 512, np.stack(moves), spare]), BF)
+    return jnp.asarray(np.concatenate([half_weaver()[None], forth, forth.transpose(0, 2, 1) / 512, np.stack(moves), spare]), BF)
 
 
 def dot(a, b):
@@ -91,7 +91,7 @@
 def kernel(
     order, order_row, green, sigma, screened, tables, out,
     g, s, raw, mv, cols, first, gbuf, woven, half_woven, stage, got1, got2, sig, acc,
-    half_stage, half_got, last_got, load_sem, send1, recv1, send2, recv2, half_sem, out_sem,
+    half_stage, half_got, last_got, load_sem, send1, recv1, send2, recv2, half_sem,
 ):
     e = lax.axis_index("energy")
     m = lax.axis_index("momentum")
@@ -125,10 +125,14 @@
             pltpu.make_async_copy(sigma.at[pt], s.at[pt], load_sem.at[4 + pt]),
         )
 
-    late = pltpu.make_async_copy(tables.at[pl.ds(0, MATRICES)], mv, load_sem.at[8])
+    soon = pltpu.make_async_copy(tables.at[0], mv.at[0], load_sem.at[9])
+    rest = pl.ds(1, MATRICES - 1)
+    late = pltpu.make_async_copy(tables.at[rest], mv.at[rest], load_sem.at[8])
     for pt in range(4):
         for copy in load_point(pt):
             copy.start()
+        if pt == 0:
+            soon.start()
     late.start()
 
     barrier = pltpu.get_barrier_semaphore()
@@ -166,7 +170,7 @@
                 at = (2 * part + chunk) * WIDE
                 gbuf[2 * chunk + part] = early[:, at : at + WIDE]
         if pt == 0:
-            late.wait()
+            soon.wait()
 
         def early_weave(group, _):
             both = [
@@ -230,6 +234,7 @@
         got1[chunk, me] = woven[order[me]]
         return 0
 
+    late.wait()
     lax.fori_loop(2, CHUNKS, outward, 0)
 
     lane = lax.broadcasted_iota(jnp.int32, (128, 512), 1)
@@ -383,9 +388,8 @@
                 acc[pt] = total
             else:
                 total = total.astype(BF)
-                s[pt, 0] = total[:, :512]
-                s[pt, 1] = total[:, 512:]
-                pltpu.make_async_copy(s.at[pt], out.at[pt], out_sem.at[pt]).start()
+                out[pt, 0] = total[:, :512]
+                out[pt, 1] = total[:, 512:]
             return 0
 
         return at_point
@@ -427,8 +431,6 @@
         pltpu.make_async_copy(stage.at[chunk, some], got2.at[chunk, some], send2.at[chunk]).wait()
     for half in range(2):
         whole(half, 8).wait()
-    for pt in range(4):
-        pltpu.make_async_copy(s.at[pt], out.at[pt], out_sem.at[pt]).wait()
 
 
 def local(green_ret, sigma_in, screened, block_of_slot):
@@ -440,7 +442,7 @@
         out_shape=jax.ShapeDtypeStruct((4, 2, 512, 512), BF),
         in_specs=[pl.BlockSpec(memory_space=pltpu.SMEM), pl.BlockSpec(memory_space=pltpu.VMEM)]
         + [hbm] * 4,
-        out_specs=pl.BlockSpec(memory_space=pl.ANY),
+        out_specs=pl.BlockSpec(memory_space=pltpu.VMEM),
         scratch_shapes=[
             pltpu.VMEM((4, 2, 512, 512), BF),
             pltpu.VMEM((4, 2, 512, 512), BF),
@@ -465,7 +467,6 @@
             pltpu.SemaphoreType.DMA((CHUNKS,)),
             pltpu.SemaphoreType.DMA((CHUNKS,)),
             pltpu.SemaphoreType.DMA((12,)),
-            pltpu.SemaphoreType.DMA((4,)),
         ],
         compiler_params=pltpu.CompilerParams(
             collective_id=0, has_side_effects=True, vmem_limit_bytes=48 << 20

time: 113 us -> 112 us (level)
  no operation moved by 1% of the time
where the time goes in v6:
time: 112 us
  Pallas kernels  109 us (97%)
  local copies, waits for them, and re-layouts  2.67 us (2%)
    pallas_call x1, Pallas kernels, local(): pl.pallas_call(kernel, out_shape=jax.ShapeDtypeStruct((4, 2, 512, 512), B...  109 us
    unnamed x3, local copies, waits for them, and re-layouts  2.67 us

profile of v6, /device:TPU:1, one launch (start us, length us, event | category | flops | bytes accessed | tf_op | source)
XLA Modules:
  0.0 111.6 jit_solution(3779803894066170203)
XLA Ops:
  0.0 0.0 copy-start
  0.0 0.7 copy-done
  0.7 108.9 %shard_map.55 = bf16[4,2,512,512]{3,2,1,0:T(8,128)(2,1)S(1)} custom-call(s32[128]{0:T(128)S(1)} %copy-done, s32[1,128]{1,0:T(1,128)S(1)} %bitcast.6, bf16[4,2,512,512]{3,2,1,0:T(8,128)(2,1)} %bitcast.7, bf16[4,2,512,512]{3,2,1,0:T(8,128)(2,1)} %bitcast.8, bf16[32,16,2,2048]{3,2,1,0:T(2,128)(2,1)} %bitcast.9, bf16[40,256,256]{2,1,0:T(8,128)(2,1)} %constant.2.clone.tables), custom_call_target="tpu_custom_call" | custom-call | tf_op jit(solution)/shard_map/pallas_call | solution.py:440
  109.6 2.0 %copy.7 = bf16[2,2,2,512,512]{4,3,2,1,0:T(8,128)(2,1)} copy(bf16[2,2,2,512,512]{4,3,2,1,0:T(8,128)(2,1)S(1)} %bitcast.5) | data formatting | bytes 8388608
Async XLA Ops:
  0.0 0.7 copy-start

commit v7 on v6

--- a/solution.py
+++ b/solution.py
@@ -425,7 +425,8 @@
             return 0
 
         lax.fori_loop(0, 4, half_unweave, 0)
-        lax.fori_loop(2 * half, 2 * half + 2, inward(CHUNKS - 1), 0)
+        for pt in range(2 * half, 2 * half + 2):
+            inward(CHUNKS - 1)(pt, 0)
 
     for chunk in range(CHUNKS - 1):
         pltpu.make_async_copy(stage.at[chunk, some], got2.at[chunk, some], send2.at[chunk]).wait()

time: 112 us -> 111 us (level)
  no operation moved by 1% of the time
where the time goes in v7:
time: 111 us
  Pallas kernels  108 us (97%)
  local copies, waits for them, and re-layouts  2.67 us (2%)
    pallas_call x1, Pallas kernels, local(): pl.pallas_call(kernel, out_shape=jax.ShapeDtypeStruct((4, 2, 512, 512), B...  108 us
    unnamed x3, local copies, waits for them, and re-layouts  2.67 us

profile of v7, /device:TPU:1, one launch (start us, length us, event | category | flops | bytes accessed | tf_op | source)
XLA Modules:
  0.0 110.9 jit_solution(17223409193495215117)
XLA Ops:
  0.0 0.0 copy-start
  0.0 0.7 copy-done
  0.7 108.2 %shard_map.55 = bf16[4,2,512,512]{3,2,1,0:T(8,128)(2,1)S(1)} custom-call(s32[128]{0:T(128)S(1)} %copy-done, s32[1,128]{1,0:T(1,128)S(1)} %bitcast.6, bf16[4,2,512,512]{3,2,1,0:T(8,128)(2,1)} %bitcast.7, bf16[4,2,512,512]{3,2,1,0:T(8,128)(2,1)} %bitcast.8, bf16[32,16,2,2048]{3,2,1,0:T(2,128)(2,1)} %bitcast.9, bf16[40,256,256]{2,1,0:T(8,128)(2,1)} %constant.2.clone.tables), custom_call_target="tpu_custom_call" | custom-call | tf_op jit(solution)/shard_map/pallas_call | solution.py:441
  108.9 2.0 %copy.7 = bf16[2,2,2,512,512]{4,3,2,1,0:T(8,128)(2,1)} copy(bf16[2,2,2,512,512]{4,3,2,1,0:T(8,128)(2,1)S(1)} %bitcast.5) | data formatting | bytes 8388608
Async XLA Ops:
  0.0 0.7 copy-start
